TPU v7x, 256 devices: a whole 4x4x8 slice. The times are simulated.
256 devices in a mesh: seq: 128 (over x_lo, z, y, core), head: 2 (over x_hi).
Axes of the slice: x: 4 (x_hi: 2, x_lo: 2; x = x_hi * 2 + x_lo), y: 4, z: 8, core: 2. Of those that a mesh axis runs over, the one named last changes fastest.
Arguments:
- tokens: bfloat16 [32768, 1536], P('seq', 'head'), may hold values from -8 to 8
- w_qkv: bfloat16 [1536, 3, 768], P(None, None, 'head'), may hold values from -0.15625 to 0.15625
- w_out: bfloat16 [768, 1536], P('head'), may hold values from -0.21875 to 0.21875
- grad_out: bfloat16 [32768, 1536], P('seq', 'head'), may hold values from -24 to 24
- offsets: int32 [4, 12], P(None, 'head'), may hold values from 0 to 255, as said below
Outputs:
- mixed: bfloat16 [32768, 1536], P('seq', 'head')
- grad_tokens: bfloat16 [32768, 1536], P('seq', 'head')
- grad_qkv: float32 [1536, 3, 768], P('seq', None, 'head')
- grad_w_out: float32 [768, 1536], P('head', 'seq')
Inputs may be any that keep to these rules, and one draw needn't show every extreme that they name: offsets[l, h] is below the dilation r_l of level l (1, 4, 64, 256); at every level some head takes r_l - 1.
All inputs are finite; a program needn't handle non-finite values.
Results may differ from a plain program's by a relative error of at most 0.017.
Values may be sent and summed in bfloat16 or wider, within the bound.
A program may use at most 128 MiB of HBM per device.

v0:
```python
import jax
import jax.numpy as jnp
from jax import lax
from jax.sharding import PartitionSpec as P

SCALE = 0.125


def partner(value, axis, distance):
    mask = 2**distance
    pairs = [(source, source ^ mask) for source in range(lax.axis_size(axis))]
    return lax.ppermute(value, axis, pairs)


def pick_rows(flat, dilation, column_shift):
    if dilation == 1:
        return flat
    count, columns = flat.shape
    blocks = flat.reshape(count // dilation, dilation, columns)
    hit = jnp.arange(dilation, dtype=jnp.int32)[:, None] == column_shift[None, :]
    return jnp.sum(jnp.where(hit[None], blocks, jnp.zeros((), flat.dtype)), axis=1)


def place_rows(picked, dilation, column_shift):
    if dilation == 1:
        return picked
    count, columns = picked.shape
    hit = jnp.arange(dilation, dtype=jnp.int32)[:, None] == column_shift[None, :]
    full = jnp.where(hit[None], picked[:, None, :], jnp.zeros((), picked.dtype))
    return full.reshape(count * dilation, columns)


def pick_stats(stats, dilation, shifts):
    if dilation == 1:
        return stats
    heads, count = stats.shape
    blocks = stats.reshape(heads, count // dilation, dilation)
    hit = jnp.arange(dilation, dtype=jnp.int32)[None, :] == shifts[:, None]
    return jnp.sum(jnp.where(hit[:, None, :], blocks, jnp.zeros((), stats.dtype)), axis=2)


def place_stats(picked, dilation, shifts):
    if dilation == 1:
        return picked
    heads, count = picked.shape
    hit = jnp.arange(dilation, dtype=jnp.int32)[None, :] == shifts[:, None]
    full = jnp.where(hit[:, None, :], picked[:, :, None], jnp.zeros((), picked.dtype))
    return full.reshape(heads, count * dilation)


def attend_forward(queries, pairs, heads):
    count, width = queries.shape
    head_size = width // heads
    keys = pairs[:, :width].reshape(-1, heads, head_size)
    values = pairs[:, width:].reshape(-1, heads, head_size)
    scores = (
        jnp.einsum(
            "qhe,khe->hqk",
            queries.reshape(count, heads, head_size),
            keys,
            preferred_element_type=jnp.float32,
        )
        * SCALE
    )
    weights = jnp.exp(scores)
    total = jnp.sum(weights, axis=2)
    numer = jnp.einsum(
        "hqk,khe->qhe", weights.astype(jnp.bfloat16), values, preferred_element_type=jnp.float32
    )
    return (numer.reshape(count, width), total)


def attend_backward(queries, pairs, grads, deltas, totals, heads):
    count, width = queries.shape
    head_size = width // heads
    query_heads = queries.reshape(count, heads, head_size)
    grad_heads = grads.reshape(count, heads, head_size)
    keys = pairs[:, :width].reshape(-1, heads, head_size)
    values = pairs[:, width:].reshape(-1, heads, head_size)
    scores = (
        jnp.einsum("qhe,khe->hqk", query_heads, keys, preferred_element_type=jnp.float32) * SCALE
    )
    probs = jnp.exp(scores) / totals[:, :, None]
    grad_values = jnp.einsum(
        "hqk,qhe->khe", probs.astype(jnp.bfloat16), grad_heads, preferred_element_type=jnp.float32
    )
    grad_probs = jnp.einsum("qhe,khe->hqk", grad_heads, values, preferred_element_type=jnp.float32)
    grad_scores = (probs * (grad_probs - deltas[:, :, None])).astype(jnp.bfloat16)
    grad_queries = (
        jnp.einsum("hqk,khe->qhe", grad_scores, keys, preferred_element_type=jnp.float32) * SCALE
    )
    grad_keys = (
        jnp.einsum("hqk,qhe->khe", grad_scores, query_heads, preferred_element_type=jnp.float32)
        * SCALE
    )
    key_rows = keys.shape[0]
    both = jnp.concatenate(
        [grad_keys.reshape(key_rows, width), grad_values.reshape(key_rows, width)], 1
    )
    return (grad_queries.reshape(count, width), both)


def upper_side(bit):
    return lax.axis_index("seq") // 2**bit % 2 == 1


def grow_one(block, bit):
    other = partner(block, "seq", bit)
    upper = upper_side(bit)
    return jnp.where(upper, jnp.concatenate([other, block], 0), jnp.concatenate([block, other], 0))


def shrink_one(block, bit):
    half = block.shape[0] // 2
    upper = upper_side(bit)
    outgoing = jnp.where(upper, block[:half], block[half:])
    kept = jnp.where(upper, block[half:], block[:half])
    return kept + partner(outgoing.astype(jnp.bfloat16), "seq", bit).astype(outgoing.dtype)


def per_device(tokens, w_qkv, w_out, grad_out, offsets):
    seq_count = lax.axis_size("seq")
    seq_bits = seq_count.bit_length() - 1
    whole = lax.all_gather(tokens, "head", axis=1, tiled=True)
    rows = whole.shape[0]
    local_heads = offsets.shape[1]
    width = w_out.shape[0]
    head_size = width // local_heads
    weight_flat = w_qkv.reshape(w_qkv.shape[0], 3 * width)
    projected = jnp.dot(whole, weight_flat, preferred_element_type=jnp.float32).astype(jnp.bfloat16)
    queries = projected[:, :width]
    key_value = projected[:, width:]
    table = [(0, 1), (2, 4), (seq_bits - 1, seq_count // 2), (seq_bits, 2 * seq_count)]
    spread_levels = [1, 2, 3]
    query_cols = []
    pair_cols = []
    for level in range(len(table)):
        column_shift = jnp.repeat(offsets[level], head_size)
        query_cols.append(column_shift)
        pair_cols.append(jnp.concatenate([column_shift, column_shift], 0))
    picked = []
    for level, (depth, dilation) in enumerate(table):
        picked.append(pick_rows(key_value, dilation, pair_cols[level]))
    grown = list(picked)
    for level in spread_levels:
        for bit in range(table[level][0]):
            grown[level] = grow_one(grown[level], bit)
    numer = jnp.zeros((rows, width), jnp.float32)
    denom = jnp.zeros((local_heads, rows), jnp.float32)
    for level, (depth, dilation) in enumerate(table):
        shifts = offsets[level]
        chosen = pick_rows(queries, dilation, query_cols[level])
        part_num, part_den = attend_forward(chosen, grown[level], local_heads)
        numer = numer + place_rows(part_num, dilation, query_cols[level])
        denom = denom + place_stats(part_den, dilation, shifts)
    denom_cols = jnp.repeat(jnp.transpose(denom), head_size, axis=1)
    attended = (numer / denom_cols).astype(jnp.bfloat16)
    mixed = lax.psum_scatter(
        jnp.dot(attended, w_out, preferred_element_type=jnp.float32),
        "head",
        scatter_dimension=1,
        tiled=True,
    ).astype(jnp.bfloat16)
    grad_whole = lax.all_gather(grad_out, "head", axis=1, tiled=True)
    out_term = lax.dot_general(
        attended, grad_whole, (((0,), (0,)), ((), ())), preferred_element_type=jnp.float32
    )
    grad_w_out = lax.psum_scatter(out_term, "seq", scatter_dimension=1, tiled=True)
    grad_att = lax.dot_general(
        grad_whole, w_out, (((1,), (1,)), ((), ())), preferred_element_type=jnp.float32
    )
    grad_att = grad_att.astype(jnp.bfloat16)
    products = (grad_att.astype(jnp.float32) * attended.astype(jnp.float32)).reshape(
        rows, local_heads, head_size
    )
    deltas = jnp.transpose(jnp.sum(products, axis=2))
    grad_q = jnp.zeros((rows, width), jnp.float32)
    key_terms = []
    for level, (depth, dilation) in enumerate(table):
        shifts = offsets[level]
        part_q, part_kv = attend_backward(
            pick_rows(queries, dilation, query_cols[level]),
            grown[level],
            pick_rows(grad_att, dilation, query_cols[level]),
            pick_stats(deltas, dilation, shifts),
            pick_stats(denom, dilation, shifts),
            local_heads,
        )
        grad_q = grad_q + place_rows(part_q, dilation, query_cols[level])
        key_terms.append(part_kv)
    returned = list(key_terms)
    for level in spread_levels:
        for bit in reversed(range(table[level][0])):
            returned[level] = shrink_one(returned[level], bit)
    grad_kv = jnp.zeros((rows, 2 * width), jnp.float32)
    for level, (depth, dilation) in enumerate(table):
        grad_kv = grad_kv + place_rows(returned[level], dilation, pair_cols[level])
    grads_qkv = jnp.concatenate([grad_q.astype(jnp.bfloat16), grad_kv.astype(jnp.bfloat16)], 1)
    token_term = lax.dot_general(
        grads_qkv, weight_flat, (((1,), (1,)), ((), ())), preferred_element_type=jnp.float32
    )
    grad_tokens = lax.psum_scatter(token_term, "head", scatter_dimension=1, tiled=True).astype(
        jnp.bfloat16
    )
    grad_qkv = lax.psum_scatter(
        lax.dot_general(
            whole, grads_qkv, (((0,), (0,)), ((), ())), preferred_element_type=jnp.float32
        ),
        "seq",
        scatter_dimension=0,
        tiled=True,
    )
    grad_qkv = grad_qkv.reshape(grad_qkv.shape[0], 3, width)
    return (mixed, grad_tokens, grad_qkv, grad_w_out)


def solution(mesh):
    placed = (
        P("seq", "head"),
        P(None, None, "head"),
        P("head", None),
        P("seq", "head"),
        P(None, "head"),
    )
    return jax.shard_map(
        per_device,
        mesh=mesh,
        in_specs=placed,
        out_specs=(P("seq", "head"), P("seq", "head"), P("seq", None, "head"), P("head", "seq")),
        check_vma=False,
    )
```

profile of v0, /device:TPU:1, one launch (start us, length us, event | category | flops | bytes accessed | tf_op | source)
XLA Modules:
  0.0 1405.0 jit_solution(12976139266028696167)
XLA Ops:
  9.1 12.3 all_gather.6
  21.4 6.4 copy.208
  27.8 3.2 convolution_convert_fusion
  31.7 14.7 %collective-permute-start.2 = (bf16[4,768]{1,0:T(4,128)(2,1)}, bf16[4,768]{1,0:T(4,128)(2,1)}, u32[]{:S(2)}, u32[]{:S(2)}) collective-permute-start(bf16[4,768]{1,0:T(4,128)(2,1)} %select_reduce_fusion), channel_id=1, source_target_pairs={{0,2},{2,0},{4,6},{6,4},{8,10},{10,8},{12,14},{14,12},{16,18},{18,... | collective-permute-start | bytes 18440 | tf_op jit(solution)/shard_map/ppermute | solution.py:12
  47.3 11.8 collective-permute-start.8
  65.7 12.9 all_gather.7
  113.4 5.0 collective-permute-start.13
  125.4 3.7 collective-permute-start.7
  195.8 7.7 collective-permute-done.24
  204.2 10.1 collective-permute-done.25
  215.0 4.9 collective-permute-done.26
  220.9 4.3 collective-permute-start.27
  230.6 14.1 %collective-permute-start.28 = (bf16[2,768]{0,1:T(8,128)(2,1)S(1)}, bf16[2,768]{0,1:T(8,128)(2,1)S(1)}, u32[]{:S(2)}, u32[]{:S(2)}) collective-permute-start(bf16[2,768]{0,1:T(8,128)(2,1)S(1)} %select_convert_fusion.1), channel_id=1, source_target_pairs={{0,4},{2,6},{4,0},{6,2},{8,12},{10,14},{12,8},{14,10},{16,20},{18,... | collective-permute-start | bytes 9224 | tf_op jit(solution)/shard_map/ppermute | solution.py:12
  244.8 6.3 collective-permute-start.17
  255.1 7.3 collective-permute-start.18
  262.7 3.3 collective-permute-done.18
  277.6 3.2 collective-permute-start.22
  288.4 4.1 convolution_bitcast_fusion
  293.1 315.8 %fusion = f32[384,16]{0,1:T(8,128)S(1)} fusion(f32[384,1536]{0,1:T(8,128)S(1)} %fusion.70), kind=kCustom, calls=%all-reduce-scatter | all-reduce-scatter fusion | flops 786433 | bytes 2384896
  610.2 8.6 collective-permute-start.61
  628.0 10.5 collective-permute-start.52
  638.5 5.0 collective-permute-start.51
  652.5 4.3 collective-permute-start.46
  665.3 4.0 collective-permute-start.41
  669.3 3.5 collective-permute-start.40
  680.3 3.9 collective-permute-start.35
  687.3 5.4 collective-permute-start.33
  692.8 13.1 collective-permute-start.32
  705.9 13.1 collective-permute-start.31
  719.1 13.1 collective-permute-start.30
  734.9 3.8 concatenate.152
  743.2 651.7 %all-reduce.5.cloned.1.call-done = f32[1536,1152]{0,1:T(8,128)} async-done(((f32[1536,1152]{0,1:T(8,128)}), f32[1536,1152]{0,1:T(8,128)}) %all-reduce.5.cloned.1.call-update) | async-done | bytes 7077904
  (408 shorter events, 195.1 us)
Async XLA Ops:
  8.0 731.3 %reduce-scatter.6.cloned.1.call-start = ((), (), s32[]{:S(2)}) async-start(), calls=%async_computation.2 | async-start | bytes 2359296 | tf_op jit(solution)/shard_map/reduce_scatter | solution.py:158
  31.7 72.1 %collective-permute-start.2 = (bf16[4,768]{1,0:T(4,128)(2,1)}, bf16[4,768]{1,0:T(4,128)(2,1)}, u32[]{:S(2)}, u32[]{:S(2)}) collective-permute-start(bf16[4,768]{1,0:T(4,128)(2,1)} %select_reduce_fusion), channel_id=1, source_target_pairs={{0,2},{2,0},{4,6},{6,4},{8,10},{10,8},{12,14},{14,12},{16,18},{18,... | collective-permute-start | bytes 18440 | tf_op jit(solution)/shard_map/ppermute | solution.py:12
  47.3 38.9 %collective-permute-start.8 = (bf16[1,768]{1,0:T(2,128)(2,1)}, bf16[1,768]{1,0:T(2,128)(2,1)}, u32[]{:S(2)}, u32[]{:S(2)}) collective-permute-start(bf16[1,768]{1,0:T(2,128)(2,1)} %reduce_sum.232), channel_id=1, source_target_pairs={{0,2},{2,0},{4,6},{6,4},{8,10},{10,8},{12,14},{14,12},{16,18},{18,... | collective-permute-start | bytes 4616 | tf_op jit(solution)/shard_map/ppermute | solution.py:12
  60.5 61.7 %collective-permute-start = (bf16[64,768]{1,0:T(8,128)(2,1)}, bf16[64,768]{1,0:T(8,128)(2,1)}, u32[]{:S(2)}, u32[]{:S(2)}) collective-permute-start(bf16[64,768]{1,0:T(8,128)(2,1)} %select_reduce_fusion.1), channel_id=1, source_target_pairs={{0,2},{2,0},{4,6},{6,4},{8,10},{10,8},{12,14},{14,12},{16,18},{18,... | collective-permute-start | bytes 294920 | tf_op jit(solution)/shard_map/ppermute | solution.py:12
  87.0 14.7 %collective-permute-start.9 = (bf16[2,768]{1,0:T(2,128)(2,1)S(1)}, bf16[2,768]{1,0:T(2,128)(2,1)S(1)}, u32[]{:S(2)}, u32[]{:S(2)}) collective-permute-start(bf16[2,768]{1,0:T(2,128)(2,1)S(1)} %broadcast_select_fusion.8), channel_id=1, source_target_pairs={{0,4},{2,6},{4,0},{6,2},{8,12},{10,14},{12,8},{14,10},{16,20},{18,... | collective-permute-start | bytes 9224 | tf_op jit(solution)/shard_map/ppermute | solution.py:12
  125.4 21.4 %collective-permute-start.7 = (bf16[128,768]{1,0:T(8,128)(2,1)}, bf16[128,768]{1,0:T(8,128)(2,1)}, u32[]{:S(2)}, u32[]{:S(2)}) collective-permute-start(bf16[128,768]{1,0:T(8,128)(2,1)} %maximum_select_fusion.3), channel_id=1, source_target_pairs={{0,64},{2,66},{4,68},{6,70},{8,72},{10,74},{12,76},{14,78},{16,80}... | collective-permute-start | bytes 589832 | tf_op jit(solution)/shard_map/ppermute | solution.py:12
  190.0 551.4 %reduce-scatter.8.cloned.1.call-start = ((), (), s32[]{:S(2)}) async-start(), calls=%async_computation.3 | async-start | bytes 2359296 | tf_op jit(solution)/shard_map/reduce_scatter | solution.py:202
  229.0 37.2 %collective-permute-start.15 = (bf16[128,768]{0,1:T(8,128)(2,1)S(1)}, bf16[128,768]{0,1:T(8,128)(2,1)}, u32[]{:S(2)}, u32[]{:S(2)}) collective-permute-start(bf16[128,768]{0,1:T(8,128)(2,1)S(1)} %select_convert_fusion.9), channel_id=1, source_target_pairs={{0,4},{2,6},{4,0},{6,2},{8,12},{10,14},{12,8},{14,10},{16,20},{18,... | collective-permute-start | bytes 589832 | tf_op jit(solution)/shard_map/ppermute | solution.py:12
  230.6 20.5 %collective-permute-start.28 = (bf16[2,768]{0,1:T(8,128)(2,1)S(1)}, bf16[2,768]{0,1:T(8,128)(2,1)S(1)}, u32[]{:S(2)}, u32[]{:S(2)}) collective-permute-start(bf16[2,768]{0,1:T(8,128)(2,1)S(1)} %select_convert_fusion.1), channel_id=1, source_target_pairs={{0,4},{2,6},{4,0},{6,2},{8,12},{10,14},{12,8},{14,10},{16,20},{18,... | collective-permute-start | bytes 9224 | tf_op jit(solution)/shard_map/ppermute | solution.py:12
  287.2 1107.7 %all-reduce.5.cloned.1.call-start = ((), (), s32[]{:S(2)}) async-start(), calls=%async_computation.4 | async-start | bytes 14155776
  608.9 15.2 %collective-permute-start.60 = (f32[384,16]{0,1:T(8,128)S(1)}, f32[384,16]{0,1:T(8,128)S(1)}, u32[]{:S(2)}, u32[]{:S(2)}) collective-permute-start(f32[384,16]{0,1:T(8,128)S(1)} %fusion), channel_id=1, source_target_pairs={{0,62},{2,64},{4,66},{6,68},{8,70},{10,72},{12,74},{14,76},{16,78}... | collective-permute-start | bytes 73736
  622.8 15.7 %collective-permute-start.56 = (f32[384,16]{0,1:T(8,128)S(1)}, f32[384,16]{0,1:T(8,128)S(1)}, u32[]{:S(2)}, u32[]{:S(2)}) collective-permute-start(f32[384,16]{0,1:T(8,128)S(1)} %fusion), channel_id=1, source_target_pairs={{0,54},{2,56},{4,58},{6,60},{8,62},{10,64},{12,66},{14,68},{16,70}... | collective-permute-start | bytes 73736
  624.1 19.4 %collective-permute-start.55 = (f32[384,16]{0,1:T(8,128)S(1)}, f32[384,16]{0,1:T(8,128)S(1)}, u32[]{:S(2)}, u32[]{:S(2)}) collective-permute-start(f32[384,16]{0,1:T(8,128)S(1)} %fusion), channel_id=1, source_target_pairs={{0,52},{2,54},{4,56},{6,58},{8,60},{10,62},{12,64},{14,66},{16,68}... | collective-permute-start | bytes 73736
  625.4 21.0 %collective-permute-start.54 = (f32[384,16]{0,1:T(8,128)S(1)}, f32[384,16]{0,1:T(8,128)S(1)}, u32[]{:S(2)}, u32[]{:S(2)}) collective-permute-start(f32[384,16]{0,1:T(8,128)S(1)} %fusion), channel_id=1, source_target_pairs={{0,50},{2,52},{4,54},{6,56},{8,58},{10,60},{12,62},{14,64},{16,66}... | collective-permute-start | bytes 73736
  626.7 22.5 %collective-permute-start.53 = (f32[384,16]{0,1:T(8,128)S(1)}, f32[384,16]{0,1:T(8,128)S(1)}, u32[]{:S(2)}, u32[]{:S(2)}) collective-permute-start(f32[384,16]{0,1:T(8,128)S(1)} %fusion), channel_id=1, source_target_pairs={{0,48},{2,50},{4,52},{6,54},{8,56},{10,58},{12,60},{14,62},{16,64}... | collective-permute-start | bytes 73736
  628.0 23.1 %collective-permute-start.52 = (f32[384,16]{0,1:T(8,128)S(1)}, f32[384,16]{0,1:T(8,128)S(1)}, u32[]{:S(2)}, u32[]{:S(2)}) collective-permute-start(f32[384,16]{0,1:T(8,128)S(1)} %fusion), channel_id=1, source_target_pairs={{0,46},{2,48},{4,50},{6,52},{8,54},{10,56},{12,58},{14,60},{16,62}... | collective-permute-start | bytes 73736
  638.5 14.0 collective-permute-start.51
  643.6 13.2 collective-permute-start.50
  652.5 12.8 collective-permute-start.46
  658.9 13.9 collective-permute-start.44
  660.2 13.9 collective-permute-start.43
  662.5 14.1 %collective-permute-start.42 = (f32[384,16]{0,1:T(8,128)S(1)}, f32[384,16]{0,1:T(8,128)S(1)}, u32[]{:S(2)}, u32[]{:S(2)}) collective-permute-start(f32[384,16]{0,1:T(8,128)S(1)} %fusion), channel_id=1, source_target_pairs={{0,26},{2,28},{4,30},{6,32},{8,34},{10,36},{12,38},{14,40},{16,42}... | collective-permute-start | bytes 73736
  665.3 12.9 collective-permute-start.41
  674.1 13.2 collective-permute-start.38
  676.6 16.2 %collective-permute-start.37 = (f32[384,16]{0,1:T(8,128)S(1)}, f32[384,16]{0,1:T(8,128)S(1)}, u32[]{:S(2)}, u32[]{:S(2)}) collective-permute-start(f32[384,16]{0,1:T(8,128)S(1)} %fusion), channel_id=1, source_target_pairs={{0,16},{2,18},{4,20},{6,22},{8,24},{10,26},{12,28},{14,30},{16,32}... | collective-permute-start | bytes 73736
  678.2 27.7 %collective-permute-start.36 = (f32[384,16]{0,1:T(8,128)S(1)}, f32[384,16]{0,1:T(8,128)S(1)}, u32[]{:S(2)}, u32[]{:S(2)}) collective-permute-start(f32[384,16]{0,1:T(8,128)S(1)} %fusion), channel_id=1, source_target_pairs={{0,14},{2,16},{4,18},{6,20},{8,22},{10,24},{12,26},{14,28},{16,30}... | collective-permute-start | bytes 73736
  680.3 38.8 %collective-permute-start.35 = (f32[384,16]{0,1:T(8,128)S(1)}, f32[384,16]{0,1:T(8,128)S(1)}, u32[]{:S(2)}, u32[]{:S(2)}) collective-permute-start(f32[384,16]{0,1:T(8,128)S(1)} %fusion), channel_id=1, source_target_pairs={{0,12},{2,14},{4,16},{6,18},{8,20},{10,22},{12,24},{14,26},{16,28}... | collective-permute-start | bytes 73736
  684.2 49.9 %collective-permute-start.34 = (f32[384,16]{0,1:T(8,128)S(1)}, f32[384,16]{0,1:T(8,128)S(1)}, u32[]{:S(2)}, u32[]{:S(2)}) collective-permute-start(f32[384,16]{0,1:T(8,128)S(1)} %fusion), channel_id=1, source_target_pairs={{0,10},{2,12},{4,14},{6,16},{8,18},{10,20},{12,22},{14,24},{16,26}... | collective-permute-start | bytes 73736
  687.3 46.8 %collective-permute-start.33 = (f32[384,16]{0,1:T(8,128)S(1)}, f32[384,16]{0,1:T(8,128)S(1)}, u32[]{:S(2)}, u32[]{:S(2)}) collective-permute-start(f32[384,16]{0,1:T(8,128)S(1)} %fusion), channel_id=1, source_target_pairs={{0,8},{2,10},{4,12},{6,14},{8,16},{10,18},{12,20},{14,22},{16,24},... | collective-permute-start | bytes 73736
  692.8 41.3 %collective-permute-start.32 = (f32[384,16]{0,1:T(8,128)S(1)}, f32[384,16]{0,1:T(8,128)S(1)}, u32[]{:S(2)}, u32[]{:S(2)}) collective-permute-start(f32[384,16]{0,1:T(8,128)S(1)} %fusion), channel_id=1, source_target_pairs={{0,6},{2,8},{4,10},{6,12},{8,14},{10,16},{12,18},{14,20},{16,22},{... | collective-permute-start | bytes 73736
  705.9 28.2 %collective-permute-start.31 = (f32[384,16]{0,1:T(8,128)S(1)}, f32[384,16]{0,1:T(8,128)S(1)}, u32[]{:S(2)}, u32[]{:S(2)}) collective-permute-start(f32[384,16]{0,1:T(8,128)S(1)} %fusion), channel_id=1, source_target_pairs={{0,4},{2,6},{4,8},{6,10},{8,12},{10,14},{12,16},{14,18},{16,20},{1... | collective-permute-start | bytes 73736
  719.1 15.8 %collective-permute-start.30 = (f32[384,16]{0,1:T(8,128)S(1)}, f32[384,16]{0,1:T(8,128)S(1)}, u32[]{:S(2)}, u32[]{:S(2)}) collective-permute-start(f32[384,16]{0,1:T(8,128)S(1)} %fusion), channel_id=1, source_target_pairs={{0,2},{2,4},{4,6},{6,8},{8,10},{10,12},{12,14},{14,16},{16,18},{18... | collective-permute-start | bytes 73736
  (91 other events, 2082.7 us)
Sparse Core Ops, SparseCore 0:
  190.1 35.0 reduce-scatter.5
  287.3 33.9 reduce-scatter.7
Sparse Core Ops, SparseCore 1:
  292.6 1102.3 all-reduce.4
where the time goes:
time: 1420 us; the launch traced here: 1400 us
  waiting for transfers between devices  690 us (49%)
  blocking collectives  341 us (24%)
  starting transfers between devices  217 us (15%)
  local copies, waits for them, and re-layouts  60.5 us (4%)
  other arithmetic  41.9 us (3%)
  matrix products  35.9 us (3%)
  between operations  18.6 us (1%)
    unnamed x36, waiting for transfers between devices  653 us
    unnamed x1, blocking collectives  316 us
    unnamed x33, starting transfers between devices  123 us
    ppermute x30, starting transfers between devices, partner(): return lax.ppermute(value, axis, pairs)  94.1 us
    ppermute x30, waiting for transfers between devices, partner(): return lax.ppermute(value, axis, pairs)  37.5 us
  transfers between devices with their start and end apart: 65, of which 17 were waited for; matrix products, arithmetic and copies ran while one was open for 28% of the time, Pallas kernels for 0%

commit v1 on v0

v1 whole, which is shorter than its diff:
```python
import jax
import jax.numpy as jnp
import numpy as np
from jax import lax
from jax.experimental import pallas as pl
from jax.experimental.pallas import tpu as pltpu
from jax.sharding import PartitionSpec as P

MESH = pl.DeviceIdType.MESH
BF = jnp.bfloat16
F32 = jnp.float32
ROWS = 256
WIDTH = 384
HALF = 768
HEADS = 6
SCALE = 0.125

NN = (((1,), (0,)), ((), ()))
NT = (((1,), (1,)), ((), ()))
TN = (((0,), (0,)), ((), ()))


def mm(a, b, dims=NN):
    return lax.dot_general(a, b, dims, preferred_element_type=F32)


def iota(shape, dim):
    return lax.broadcasted_iota(jnp.int32, shape, dim)


def halves(x):
    high = x.astype(BF)
    return high, (x - high.astype(F32)).astype(BF)


def place(spread, x):
    high, low = halves(x)
    return mm(spread, high) + mm(spread, low)


def by_head(pieces):
    lanes = iota((1, pieces[0].shape[1]), 1)
    lanes = jnp.where(lanes >= WIDTH, lanes - WIDTH, lanes)
    out = pieces[0]
    for h in range(1, HEADS):
        out = jnp.where(lanes >= 64 * h, pieces[h], out)
    return out


def block_mask(rows_per_head):
    rows = HEADS * rows_per_head
    head = iota((rows, WIDTH), 0) // rows_per_head
    return head == iota((rows, WIDTH), 1) // 64


def level_forward(q_block, keys, values, own_lanes, mask):
    weights = jnp.exp(mm(q_block, keys, NT))
    if mask is not None:
        weights = jnp.where(mask, weights, 0.0)
    total = jnp.sum(weights, axis=1, keepdims=True)
    numer = mm(weights.astype(BF), values)
    both = jnp.concatenate(
        [jnp.where(own_lanes, numer, 0.0), jnp.where(own_lanes, total, 0.0)], 1
    )
    return weights, both


def level_backward(weights, q_block, grad_block, keys, values, inverse, delta, own_lanes):
    probs = weights * inverse
    grad_probs = mm(grad_block, values, NT)
    grad_scores = (probs * (grad_probs - delta)).astype(BF)
    grad_values = mm(probs.astype(BF), grad_block, TN)
    grad_keys = mm(grad_scores, q_block, TN)
    grad_q = jnp.where(own_lanes, mm(grad_scores, keys) * SCALE, 0.0)
    return grad_q, jnp.concatenate([grad_keys, grad_values], 1)


def kernel(
    tok_hbm, gout_hbm, wqkv_hbm, wout_hbm, perm_hbm, comp_hbm, off_ref,
    mixed_ref, gtok_ref, gqkv_ref, gwout_ref,
    tok, gout, wqkv, wout, perm, comp, sib_tok, sib_gout,
    acc, qkv, kv1, s1, kv23, w0, w1, w23, numer_ref, den_ref, gatt, att_buf, gq_acc, gkv_acc,
    tok_t, gout_t, gbuf, gsend1, grecv1, gsendz, grecvz, gsends, grecvs,
    mixed_out, mixed_in, gtok_out, gtok_in,
    ysend, yrecv, zsend, zrecv, xbuf, xrecv,
    local_sem, head_s, head_r, sib_s, sib_r, k1_s, k1_r, s1_s, s1_r, kz_s, kz_r,
    r1_s, r1_r, rz_s, rz_r, rs_s, rs_r, y_s, y_r, z_s, z_r, x_s, x_r,
):
    seq = lax.axis_index("seq")
    head = lax.axis_index("head")

    def bit(step):
        return lax.rem(lax.div(seq, step), 2)

    core = bit(1)
    y_at = lax.rem(lax.div(seq, 2), 4)
    z_at = lax.rem(lax.div(seq, 8), 8)
    x_at = lax.div(seq, 64)

    def flipped(d, steps):
        other = seq
        for b, step in enumerate(steps):
            if d >> b & 1:
                other = other + (1 - 2 * bit(step)) * step
        return other

    group_steps = (1, 2, 4, 64)
    z_steps = (8, 16, 32)
    group_peer = [flipped(d, group_steps) for d in range(16)]
    z_peer = [flipped(d, z_steps) for d in range(8)]
    y_peer = [flipped(d, (2, 4)) for d in range(4)]
    sibling = group_peer[1]
    other_head = 1 - head

    def push(src, dst, send, recv, to_seq, to_head=None):
        target = (to_seq, head if to_head is None else to_head)
        copy = pltpu.make_async_remote_copy(
            src_ref=src, dst_ref=dst, send_sem=send, recv_sem=recv,
            device_id=target, device_id_type=MESH,
        )
        copy.start()
        sent.append(copy)
        return copy

    sent = []

    loads = []
    for n, (src, dst) in enumerate([
        (tok_hbm, tok.at[head]), (wqkv_hbm, wqkv), (gout_hbm, gout.at[head]),
        (wout_hbm, wout), (comp_hbm, comp), (perm_hbm, perm),
    ]):
        copy = pltpu.make_async_copy(src, dst, local_sem.at[n])
        copy.start()
        loads.append(copy)

    barrier = pltpu.get_barrier_semaphore()
    peers = [(seq, other_head)]
    peers += [(group_peer[d], head) for d in range(1, 16)]
    peers += [(z_peer[d], head) for d in range(1, 8)]
    for peer in peers:
        pl.semaphore_signal(barrier, inc=1, device_id=peer, device_id_type=MESH)
    pl.semaphore_wait(barrier, len(peers))

    tok_copy = push(tok_hbm, tok.at[head], head_s.at[0], head_r.at[0], seq, other_head)
    gout_copy = push(gout_hbm, gout.at[head], head_s.at[1], head_r.at[1], seq, other_head)

    loads[0].wait()
    loads[1].wait()
    for j in range(3):
        cols = slice(WIDTH * j, WIDTH * (j + 1))
        acc[:, cols] = mm(tok[head], wqkv[j, pl.ds(pl.multiple_of(head * HALF, HALF), HALF), :])

    lane = iota((64, ROWS), 1)
    row = iota((64, ROWS), 0)
    pick1 = jnp.concatenate(
        [jnp.where(lane == 4 * row + off_ref[1, h], 1.0, 0.0) for h in range(HEADS)], 0
    ).astype(BF)
    lane8 = iota((8, ROWS), 1)
    row8 = iota((8, ROWS), 0)

    def spot(at, h):
        return jnp.where(
            at < 4, 64 * at + off_ref[2, h], jnp.where(at == 4, off_ref[3, h], -1)
        )

    pick23 = jnp.concatenate(
        [jnp.where(lane8 == spot(row8, h), 1.0, 0.0) for h in range(HEADS)], 0
    ).astype(BF)
    at1 = iota((1, WIDTH), 1)
    spot1 = 4 * at1 + off_ref[1, 0]
    for h in range(1, HEADS):
        spot1 = jnp.where(at1 >= 64 * h, 4 * (at1 - 64 * h) + off_ref[1, h], spot1)
    put1 = jnp.where(iota((ROWS, WIDTH), 0) == spot1, 1.0, 0.0).astype(BF)
    at23 = iota((1, 8 * HEADS), 1)
    spot23 = spot(at23, 0)
    for h in range(1, HEADS):
        spot23 = jnp.where(at23 >= 8 * h, spot(at23 - 8 * h, h), spot23)
    put23 = jnp.where(iota((ROWS, 8 * HEADS), 0) == spot23, 1.0, 0.0).astype(BF)
    own1 = block_mask(64)
    own23 = block_mask(8)

    tok_copy.wait_recv()
    for j in range(3):
        cols = slice(WIDTH * j, WIDTH * (j + 1))
        other_rows = pl.ds(pl.multiple_of(other_head * HALF, HALF), HALF)
        part = acc[:, cols] + mm(tok[other_head], wqkv[j, other_rows, :])
        if j == 0:
            part = part.astype(BF).astype(F32) * SCALE
        qkv[:, cols] = part.astype(BF)

    key_value = qkv[:, WIDTH:]
    picked23 = mm(pick23, key_value)
    small = by_head([picked23[8 * h : 8 * h + 8] for h in range(HEADS)])
    s1[0] = jnp.concatenate([small, jnp.zeros_like(small)], 0).astype(BF)
    s1_copies = [
        push(s1.at[0], s1.at[d], s1_s.at[d], s1_r.at[d], group_peer[d]) for d in range(1, 16)
    ]
    picked1 = mm(pick1, key_value)
    kv1[0] = by_head([picked1[64 * h : 64 * h + 64] for h in range(HEADS)]).astype(BF)
    k1_copies = [
        push(kv1.at[0], kv1.at[d], k1_s.at[d], k1_r.at[d], group_peer[d]) for d in range(1, 4)
    ]
    sib_tok_copy = push(tok.at[1 - core], sib_tok, sib_s.at[0], sib_r.at[0], sibling)

    q_block1 = jnp.where(own1, mm(pick1, qkv[:, :WIDTH]), 0.0).astype(BF)
    q_block23 = jnp.where(own23, mm(pick23, qkv[:, :WIDTH]), 0.0).astype(BF)

    low_lanes = iota((1, 128), 1) < 64
    side = [jnp.where(low_lanes, 1.0, 0.0).astype(BF), jnp.where(low_lanes, 0.0, 1.0).astype(BF)]

    def pair(start, p):
        return qkv[:, start + 128 * p : start + 128 * p + 128]

    def level0_forward(p):
        queries, keys, values = pair(0, p), pair(WIDTH, p), pair(2 * WIDTH, p)
        parts = []
        for e in range(2):
            weights = jnp.exp(mm(queries * side[e], keys, NT))
            w0[2 * p + e] = weights
            parts.append((mm(weights.astype(BF), values), jnp.sum(weights, axis=1, keepdims=True)))
        numer_ref[:, 128 * p : 128 * p + 128] = jnp.where(low_lanes, parts[0][0], parts[1][0])
        den_ref[:, 128 * p : 128 * p + 128] = jnp.where(low_lanes, parts[0][1], parts[1][1])

    level0_forward(0)

    loads[4].wait()
    for copy in s1_copies:
        copy.wait_recv()
    kv23[0] = mm(comp[...], s1[...].reshape(256, 2 * WIDTH)).astype(BF)
    kz_copies = [
        push(kv23.at[0], kv23.at[d], kz_s.at[d], kz_r.at[d], z_peer[d]) for d in range(1, 8)
    ]

    level0_forward(1)
    level0_forward(2)

    loads[2].wait()
    loads[3].wait()
    gout_copy.wait_recv()
    sib_gout_copy = push(gout.at[1 - core], sib_gout, sib_s.at[1], sib_r.at[1], sibling)
    grad_att = (mm(gout[0], wout[:, :HALF], NT) + mm(gout[1], wout[:, HALF:], NT)).astype(BF)
    gatt[...] = grad_att
    g_block1 = jnp.where(own1, mm(pick1, grad_att), 0.0).astype(BF)
    g_block23 = jnp.where(own23, mm(pick23, grad_att), 0.0).astype(BF)

    for copy in k1_copies:
        copy.wait_recv()
    keys1, values1 = kv1[:, :, :WIDTH].reshape(256, WIDTH), kv1[:, :, WIDTH:].reshape(256, WIDTH)
    weights, both = level_forward(q_block1, keys1, values1, own1, None)
    w1[...] = weights
    placed = place(put1, both)
    numer_ref[...] += placed[:, :WIDTH]
    den_ref[...] += placed[:, WIDTH:]

    loads[5].wait()
    sib_tok_copy.wait_recv()
    tok_t[:, :ROWS] = mm(perm[...], tok[core], NT).astype(BF)
    tok_t[:, ROWS:] = mm(perm[...], sib_tok[...], NT).astype(BF)

    for copy in kz_copies:
        copy.wait_recv()
    keys23 = kv23[:, :, :WIDTH].reshape(WIDTH, WIDTH)
    values23 = kv23[:, :, WIDTH:].reshape(WIDTH, WIDTH)
    small_row = lax.rem(iota((8 * HEADS, WIDTH), 0), 8)
    wide_key = lax.rem(iota((8 * HEADS, WIDTH), 1), 48) >= 32
    mask23 = jnp.where(wide_key, small_row, small_row + 8)
    mask23 = (mask23 == 4) | ((mask23 >= 8) & (mask23 < 12))
    weights, both = level_forward(q_block23, keys23, values23, own23, mask23)
    w23[...] = weights
    placed = place(put23, both)
    numer = numer_ref[...] + placed[:, :WIDTH]
    den = den_ref[...] + placed[:, WIDTH:]
    attended = (numer / den).astype(BF)
    att_buf[0] = attended
    att_copy = push(att_buf.at[0], att_buf.at[1], sib_s.at[2], sib_r.at[2], sibling)

    inverse = 1.0 / den
    products = grad_att.astype(F32) * attended.astype(F32)
    stat_lane = iota((1, 128), 1)
    stats = jnp.zeros((ROWS, 128), F32)
    inverses, deltas = [], []
    for h in range(HEADS):
        inv = inverse[:, 64 * h : 64 * h + 1]
        delta = jnp.sum(products[:, 64 * h : 64 * h + 64], axis=1, keepdims=True)
        inverses.append(inv)
        deltas.append(delta)
        stats = jnp.where(stat_lane == h, inv, stats)
        stats = jnp.where(stat_lane == 8 + h, delta, stats)
    stats = jnp.concatenate(halves(stats), 1)

    def picked_stats(pick, rows_per_head):
        rows = HEADS * rows_per_head
        got = mm(pick, stats)
        got = got[:, :128] + got[:, 128:]
        at = iota((rows, 128), 0) // rows_per_head
        lanes = iota((rows, 128), 1)
        inv = jnp.sum(jnp.where(lanes == at, got, 0.0), axis=1, keepdims=True)
        delta = jnp.sum(jnp.where(lanes == at + 8, got, 0.0), axis=1, keepdims=True)
        return inv, delta

    inv, delta = picked_stats(pick23, 8)
    grad_q23, grad_kv = level_backward(
        w23[...], q_block23, g_block23, keys23, values23, inv, delta, own23
    )
    gsendz[...] = grad_kv.astype(BF).reshape(8, 48, 2 * WIDTH)
    rz_copies = [
        push(gsendz.at[d], grecvz.at[d], rz_s.at[d], rz_r.at[d], z_peer[d]) for d in range(1, 8)
    ]

    inv, delta = picked_stats(pick1, 64)
    grad_q1, grad_kv = level_backward(
        w1[...], q_block1, g_block1, keys1, values1, inv, delta, own1
    )
    gsend1[...] = grad_kv.astype(BF).reshape(4, 64, 2 * WIDTH)
    r1_copies = [
        push(gsend1.at[d], grecv1.at[d], r1_s.at[d], r1_r.at[d], group_peer[d])
        for d in range(1, 4)
    ]
    gq_acc[...] = place(put1, grad_q1) + place(put23, grad_q23)

    def level0_backward(p):
        queries, keys, values = pair(0, p), pair(WIDTH, p), pair(2 * WIDTH, p)
        grads = gatt[:, 128 * p : 128 * p + 128]
        parts = []
        for e in range(2):
            h = 2 * p + e
            probs = w0[h] * inverses[h]
            grad_probs = mm(grads * side[e], values, NT)
            grad_scores = (probs * (grad_probs - deltas[h])).astype(BF)
            parts.append((
                mm(grad_scores, keys) * SCALE,
                mm(grad_scores, queries, TN),
                mm(probs.astype(BF), grads, TN),
            ))
        merged = [jnp.where(low_lanes, a, b) for a, b in zip(*parts)]
        cols = slice(128 * p, 128 * p + 128)
        gq_acc[:, cols] += merged[0]
        gkv_acc[:, cols] = merged[1]
        gkv_acc[:, WIDTH + 128 * p : WIDTH + 128 * p + 128] = merged[2]

    level0_backward(0)
    level0_backward(1)

    total = gsendz[0].astype(F32)
    for d in range(1, 8):
        rz_copies[d - 1].wait_recv()
        total = total + grecvz[d].astype(F32)
    gsends[...] = mm(comp[...], total.astype(BF), TN).astype(BF).reshape(16, 16, 2 * WIDTH)
    rs_copies = [
        push(gsends.at[d], grecvs.at[d], rs_s.at[d], rs_r.at[d], group_peer[d])
        for d in range(1, 16)
    ]

    level0_backward(2)
    grad_q = gq_acc[...].astype(BF)
    gbuf[0, 0] = grad_q
    gq_copy = push(gbuf.at[0, 0], gbuf.at[0, 1], sib_s.at[3], sib_r.at[3], sibling)

    sib_gout_copy.wait_recv()
    gout_t[:, :ROWS] = mm(perm[...], gout[core], NT).astype(BF)
    gout_t[:, ROWS:] = mm(perm[...], sib_gout[...], NT).astype(BF)

    def weight_terms(r, p, left, own, other):
        term = mm(left[:, :ROWS], own) + mm(left[:, ROWS:], other)
        ysend[r, :, p] = term.astype(BF).reshape(4, 192, WIDTH)

    def y_stage(r):
        copies = []
        for d in range(1, 4):
            block = lax.rem(lax.div(y_peer[d], 2), 4)
            copies.append(push(
                ysend.at[r, block], yrecv.at[r, d], y_s.at[r, d], y_r.at[r, d], y_peer[d]
            ))
        return copies

    def z_stage(r, copies):
        for copy in copies:
            copy.wait_recv()
        total = ysend[r, y_at].astype(F32)
        for d in range(1, 4):
            total = total + yrecv[r, d].astype(F32)
        for n in range(8):
            rows = slice(24 * n, 24 * n + 24)
            zsend[r, n] = jnp.concatenate([total[0, rows], total[1, rows]], 0).astype(BF)
        out = []
        for d in range(1, 8):
            block = lax.rem(lax.div(z_peer[d], 8), 8)
            out.append(push(
                zsend.at[r, block], zrecv.at[r, d], z_s.at[r, d], z_r.at[r, d], z_peer[d]
            ))
        return out

    def x_stage(r, copies):
        total = zsend[r, z_at].astype(F32)
        for d in range(1, 8):
            copies[d - 1].wait_recv()
            total = total + zrecv[r, d].astype(F32)
        xbuf[r] = total
        out = []
        for n, d in enumerate((1, 8, 9)):
            out.append(push(xbuf.at[r], xrecv.at[r, n], x_s.at[r, n], x_r.at[r, n], group_peer[d]))
        return out

    att_copy.wait_recv()
    weight_terms(0, 0, gout_t, att_buf[0], att_buf[1])
    gq_copy.wait_recv()
    weight_terms(0, 1, tok_t, gbuf[0, 0], gbuf[0, 1])
    y0 = y_stage(0)

    def tiled(x):
        return jnp.concatenate([x] * HEADS, 0)

    total = gsend1[0].astype(F32)
    for d in range(1, 4):
        r1_copies[d - 1].wait_recv()
        total = total + grecv1[d].astype(F32)
    both1 = jnp.concatenate([own1, own1], 1)
    grad_kv = gkv_acc[...] + place(put1, jnp.where(both1, tiled(total), 0.0))
    total = gsends[0].astype(F32)
    for d in range(1, 16):
        rs_copies[d - 1].wait_recv()
        total = total + grecvs[d].astype(F32)
    both23 = jnp.concatenate([own23, own23], 1)
    grad_kv = grad_kv + place(put23, jnp.where(both23, tiled(total[:8]), 0.0))
    grad_kv = grad_kv.astype(BF)
    gbuf[1, 0] = grad_kv[:, :WIDTH]
    gbuf[2, 0] = grad_kv[:, WIDTH:]
    gk_copy = push(gbuf.at[1, 0], gbuf.at[1, 1], sib_s.at[4], sib_r.at[4], sibling)
    gv_copy = push(gbuf.at[2, 0], gbuf.at[2, 1], sib_s.at[5], sib_r.at[5], sibling)

    gk_copy.wait_recv()
    weight_terms(1, 0, tok_t, gbuf[1, 0], gbuf[1, 1])
    gv_copy.wait_recv()
    weight_terms(1, 1, tok_t, gbuf[2, 0], gbuf[2, 1])
    y1 = y_stage(1)

    def token_part(which):
        rows = pl.ds(pl.multiple_of(which * HALF, HALF), HALF)
        out = mm(gbuf[0, 0], wqkv[0, rows, :], NT)
        out = out + mm(gbuf[1, 0], wqkv[1, rows, :], NT)
        return out + mm(gbuf[2, 0], wqkv[2, rows, :], NT)

    def mixed_part(which):
        return mm(att_buf[0], wout[:, pl.ds(pl.multiple_of(which * HALF, HALF), HALF)])

    gtok_out[...] = token_part(other_head).astype(BF)
    gtok_copy = push(gtok_out, gtok_in, head_s.at[2], head_r.at[2], seq, other_head)
    z0 = z_stage(0, y0)
    mixed_out[...] = mixed_part(other_head).astype(BF)
    mixed_copy = push(mixed_out, mixed_in, head_s.at[3], head_r.at[3], seq, other_head)
    own_tokens = token_part(head)
    z1 = z_stage(1, y1)
    x0 = x_stage(0, z0)
    gtok_copy.wait_recv()
    gtok_ref[...] = (own_tokens + gtok_in[...].astype(F32)).astype(BF)
    own_mixed = mixed_part(head)
    mixed_copy.wait_recv()
    mixed_ref[...] = (own_mixed + mixed_in[...].astype(F32)).astype(BF)
    x1 = x_stage(1, z1)

    def finish(r, copies):
        for copy in copies:
            copy.wait_recv()
        straight = xbuf[r] + xrecv[r, 1]
        crossed = xrecv[r, 0] + xrecv[r, 2]
        total = jnp.where(core == x_at, straight, crossed)
        return [
            jnp.where(core == 0, total[24 * n : 24 * n + 12], total[24 * n + 12 : 24 * n + 24])
            for n in range(2)
        ]

    first, second = finish(0, x0)
    gwout_ref[...] = first
    gqkv_ref[0] = second
    first, second = finish(1, x1)
    gqkv_ref[1] = first
    gqkv_ref[2] = second
    for copy in sent:
        copy.wait_send()


def constants():
    at = np.arange(HALF)
    y, z, i = at // 192, at % 192 // 24, at % 24
    perm = np.zeros((HALF, HALF), np.float32)
    perm[at, z * 96 + y * 24 + i] = 1
    comp = np.zeros((48, 256), np.float32)
    for r in range(32):
        comp[r, r // 4 * 16 + r % 4] = 1
    for d in range(16):
        comp[32 + d, 16 * d + 4] = 1
    return jnp.asarray(perm, BF), jnp.asarray(comp, BF)


def per_device(tokens, w_qkv, w_out, grad_out, offsets):
    perm, comp = constants()
    vm = pltpu.VMEM
    dma = pltpu.SemaphoreType.DMA
    scratch = [
        vm((2, ROWS, HALF), BF), vm((2, ROWS, HALF), BF), vm((3, 2 * HALF, WIDTH), BF),
        vm((WIDTH, 2 * HALF), BF), vm((HALF, HALF), BF), vm((48, 256), BF),
        vm((ROWS, HALF), BF), vm((ROWS, HALF), BF),
        vm((ROWS, 3 * WIDTH), F32), vm((ROWS, 3 * WIDTH), BF),
        vm((4, 64, 2 * WIDTH), BF), vm((16, 16, 2 * WIDTH), BF), vm((8, 48, 2 * WIDTH), BF),
        vm((HEADS, ROWS, ROWS), F32), vm((WIDTH, ROWS), F32), vm((8 * HEADS, WIDTH), F32),
        vm((ROWS, WIDTH), F32), vm((ROWS, WIDTH), F32), vm((ROWS, WIDTH), BF),
        vm((2, ROWS, WIDTH), BF), vm((ROWS, WIDTH), F32), vm((ROWS, 2 * WIDTH), F32),
        vm((HALF, 2 * ROWS), BF), vm((HALF, 2 * ROWS), BF), vm((3, 2, ROWS, WIDTH), BF),
        vm((4, 64, 2 * WIDTH), BF), vm((4, 64, 2 * WIDTH), BF),
        vm((8, 48, 2 * WIDTH), BF), vm((8, 48, 2 * WIDTH), BF),
        vm((16, 16, 2 * WIDTH), BF), vm((16, 16, 2 * WIDTH), BF),
        vm((ROWS, HALF), BF), vm((ROWS, HALF), BF), vm((ROWS, HALF), BF), vm((ROWS, HALF), BF),
        vm((2, 4, 2, 192, WIDTH), BF), vm((2, 4, 2, 192, WIDTH), BF),
        vm((2, 8, 48, WIDTH), BF), vm((2, 8, 48, WIDTH), BF),
        vm((2, 48, WIDTH), F32), vm((2, 3, 48, WIDTH), F32),
        dma((6,)), dma((4,)), dma((4,)), dma((6,)), dma((6,)), dma((4,)), dma((4,)),
        dma((16,)), dma((16,)), dma((8,)), dma((8,)), dma((4,)), dma((4,)), dma((8,)), dma((8,)),
        dma((16,)), dma((16,)), dma((2, 4)), dma((2, 4)), dma((2, 8)), dma((2, 8)),
        dma((2, 3)), dma((2, 3)),
    ]
    anywhere = pl.BlockSpec(memory_space=pl.ANY)
    inside = pl.BlockSpec(memory_space=pltpu.VMEM)
    mixed, grad_tokens, grad_qkv, grad_w_out = pl.pallas_call(
        kernel,
        out_shape=(
            jax.ShapeDtypeStruct((ROWS, HALF), BF),
            jax.ShapeDtypeStruct((ROWS, HALF), BF),
            jax.ShapeDtypeStruct((3, 12, WIDTH), F32),
            jax.ShapeDtypeStruct((12, WIDTH), F32),
        ),
        in_specs=[anywhere] * 6 + [pl.BlockSpec(memory_space=pltpu.SMEM)],
        out_specs=(inside,) * 4,
        scratch_shapes=scratch,
        compiler_params=pltpu.CompilerParams(
            collective_id=0, has_side_effects=True, vmem_limit_bytes=56 * 2**20
        ),
        cost_estimate=pl.CostEstimate(
            flops=8 * 10**9, bytes_accessed=12 * 2**20, transcendentals=600000
        ),
    )(tokens, grad_out, jnp.transpose(w_qkv, (1, 0, 2)), w_out, perm, comp, offsets)
    return mixed, grad_tokens, jnp.transpose(grad_qkv, (1, 0, 2)), jnp.transpose(grad_w_out)


def solution(mesh):
    placed = (
        P("seq", "head"),
        P(None, None, "head"),
        P("head", None),
        P("seq", "head"),
        P(None, "head"),
    )
    return jax.shard_map(
        per_device,
        mesh=mesh,
        in_specs=placed,
        out_specs=(P("seq", "head"), P("seq", "head"), P("seq", None, "head"), P("head", "seq")),
        check_vma=False,
    )
```

time: 1420 us -> 125 us (0.09); the launches traced: 1400 us -> 125 us
  waiting for transfers between devices: 690 us -> 0 us
  blocking collectives: 341 us -> 0 us
  starting transfers between devices: 217 us -> 0 us
  Pallas kernels: 0 us -> 120 us
  local copies, waits for them, and re-layouts: 60.5 us -> 4.72 us
  other arithmetic: 41.9 us -> 0 us
  matrix products: 35.9 us -> 0 us
  between operations: 18.6 us -> 0.66 us
    unnamed x36 -> x0, waiting for transfers between devices: 653 us -> none
    unnamed x1 -> x0, blocking collectives: 316 us -> none
    unnamed x33 -> x0, starting transfers between devices: 123 us -> none
    pallas_call x0 -> x1, Pallas kernels: none -> 120 us  [per_device(): pl.pallas_call(kernel, out_shape=(jax.ShapeDtypeStruct((ROWS, HALF), BF),...]
    ppermute x30 -> x0, starting transfers between devices: 94.1 us -> none  [partner(): return lax.ppermute(value, axis, pairs)]
    ppermute x30 -> x0, waiting for transfers between devices: 37.5 us -> none  [partner(): return lax.ppermute(value, axis, pairs)]
    dot_general x28 -> x0, matrix products: 35.9 us -> none  [the longest x4 5.74 us: attend_backward(): jnp.einsum('qhe,khe->hqk', grad_heads, values, preferred_element_type=jnp...]
    all_gather x2 -> x0, blocking collectives: 25.3 us -> none  [the longest x1 12.9 us: per_device(): grad_whole = lax.all_gather(grad_out, 'head', axis=1, tiled=True)]
  transfers between devices with their start and end apart: 65 -> 0, of which waited for: 17 -> 0; matrix products, arithmetic and copies ran while one was open for 28% -> 0% of each run, Pallas kernels for 0% -> 0%
where the time goes in v1:
time: 125 us
  Pallas kernels  120 us (96%)
  local copies, waits for them, and re-layouts  4.72 us (4%)
    pallas_call x1, Pallas kernels, per_device(): pl.pallas_call(kernel, out_shape=(jax.ShapeDtypeStruct((ROWS, HALF), BF),...  120 us
    unnamed x8, local copies, waits for them, and re-layouts  4.72 us

profile of v1, /device:TPU:1, one launch (start us, length us, event | category | flops | bytes accessed | tf_op | source)
XLA Modules:
  0.0 124.9 jit_solution(5910034833946842979)
XLA Ops:
  0.6 119.6 %shard_map.102 = (bf16[256,768]{1,0:T(8,128)(2,1)}, bf16[256,768]{1,0:T(8,128)(2,1)}, f32[3,12,384]{2,1,0:T(8,128)}, f32[12,384]{1,0:T(8,128)}) custom-call(bf16[256,768]{1,0:T(8,128)(2,1)} %tok_hbm.1, bf16[256,768]{1,0:T(8,128)(2,1)} %gout_hbm.1, bf16[3,1536,384]{2,1,0:T(8,128)(2,1)} %bitcast.5, bf16[384,1536]{1,0:T(8,128)(2,1)} %wout_hbm.1, ...), custom_call_target="tpu_custom_call" | custom-call | flops 8000000000 | bytes 12582912 | tf_op jit(solution)/shard_map/pallas_call | solution.py:523
  120.2 0.0 copy-start
  120.2 0.0 copy-start.1
  120.2 1.6 %copy.11 = f32[12,3,384]{2,1,0:T(4,128)} copy(f32[12,3,384]{2,0,1:T(8,128)} %bitcast.3) | data formatting | bytes 110592
  121.8 1.8 %copy.15 = bf16[256,768]{1,0:T(8,128)(2,1)} copy(bf16[256,768]{1,0:T(8,128)(2,1)} %get-tuple-element.20) | data formatting | bytes 786432
  123.6 0.0 copy-done
  123.6 0.7 copy.16
  124.3 0.0 copy-done.1
  124.3 0.6 copy.17
Async XLA Ops:
  120.2 3.4 %copy-start = (bf16[256,768]{1,0:T(8,128)(2,1)S(1)}, bf16[256,768]{1,0:T(8,128)(2,1)}, u32[]{:S(2)}) copy-start(bf16[256,768]{1,0:T(8,128)(2,1)} %get-tuple-element.21) | copy-start | bytes 1179652
  120.2 4.1 %copy-start.1 = (f32[12,384]{1,0:T(8,128)S(1)}, f32[12,384]{1,0:T(8,128)}, u32[]{:S(2)}) copy-start(f32[12,384]{1,0:T(8,128)} %get-tuple-element.11) | copy-start | bytes 55300

commit v2 on v1

--- a/solution.py
+++ b/solution.py
@@ -79,12 +79,13 @@
     tok_hbm, gout_hbm, wqkv_hbm, wout_hbm, perm_hbm, comp_hbm, off_ref,
     mixed_ref, gtok_ref, gqkv_ref, gwout_ref,
     tok, gout, wqkv, wout, perm, comp, sib_tok, sib_gout,
-    acc, qkv, kv1, s1, kv23, w0, w1, w23, numer_ref, den_ref, gatt, att_buf, gq_acc, gkv_acc,
-    tok_t, gout_t, gbuf, gsend1, grecv1, gsendz, grecvz, gsends, grecvs,
-    mixed_out, mixed_in, gtok_out, gtok_in,
-    ysend, yrecv, zsend, zrecv, xbuf, xrecv,
-    local_sem, head_s, head_r, sib_s, sib_r, k1_s, k1_r, s1_s, s1_r, kz_s, kz_r,
-    r1_s, r1_r, rz_s, rz_r, rs_s, rs_r, y_s, y_r, z_s, z_r, x_s, x_r,
+    acc, qkv, kv1, sv, sv_in, kvz, kvh, w0, w1, w23, numer_ref, den_ref, gatt, att_buf,
+    gq_acc, gkv_acc, tok_t, gout_t, gbuf, gsend1, grecv1, gs, gs_in, gx, gx_in, gz, gz_in,
+    gf, gf_in, mixed_out, mixed_in, gtok_out, gtok_in, part_a,
+    ysend, yrecv, ysend_a, yrecv_a, ysend_b, yrecv_b, zsend, zrecv, zsend_a, zrecv_a,
+    zsend_b, zrecv_b, xbuf, xrecv,
+    local_sem, head_s, head_r, sib_s, sib_r, k1_s, k1_r, kz_s, kz_r, kx_s, kx_r,
+    r1_s, r1_r, rx_s, rx_r, rz_s, rz_r, y_s, y_r, z_s, z_r, x_s, x_r,
 ):
     seq = lax.axis_index("seq")
     head = lax.axis_index("head")
@@ -104,12 +105,11 @@
                 other = other + (1 - 2 * bit(step)) * step
         return other
 
-    group_steps = (1, 2, 4, 64)
-    z_steps = (8, 16, 32)
-    group_peer = [flipped(d, group_steps) for d in range(16)]
-    z_peer = [flipped(d, z_steps) for d in range(8)]
-    y_peer = [flipped(d, (2, 4)) for d in range(4)]
-    sibling = group_peer[1]
+    z_peer = [flipped(d, (8, 16, 32)) for d in range(8)]
+    chip_peer = [flipped(d, (2, 4, 64)) for d in range(8)]
+    pair_peer = [flipped(d, (1, 2)) for d in range(4)]
+    cross_peer = [flipped(d, (1, 64)) for d in range(4)]
+    sibling = pair_peer[1]
     other_head = 1 - head
 
     def push(src, dst, send, recv, to_seq, to_head=None):
@@ -135,14 +135,14 @@
 
     barrier = pltpu.get_barrier_semaphore()
     peers = [(seq, other_head)]
-    peers += [(group_peer[d], head) for d in range(1, 16)]
+    peers += [(sibling, head), (pair_peer[3], head), (cross_peer[3], head)]
+    peers += [(chip_peer[d], head) for d in range(1, 8)]
     peers += [(z_peer[d], head) for d in range(1, 8)]
     for peer in peers:
         pl.semaphore_signal(barrier, inc=1, device_id=peer, device_id_type=MESH)
     pl.semaphore_wait(barrier, len(peers))
 
     tok_copy = push(tok_hbm, tok.at[head], head_s.at[0], head_r.at[0], seq, other_head)
-    gout_copy = push(gout_hbm, gout.at[head], head_s.at[1], head_r.at[1], seq, other_head)
 
     loads[0].wait()
     loads[1].wait()
@@ -180,6 +180,7 @@
     own23 = block_mask(8)
 
     tok_copy.wait_recv()
+    gout_copy = push(gout_hbm, gout.at[head], head_s.at[1], head_r.at[1], seq, other_head)
     for j in range(3):
         cols = slice(WIDTH * j, WIDTH * (j + 1))
         other_rows = pl.ds(pl.multiple_of(other_head * HALF, HALF), HALF)
@@ -191,16 +192,24 @@
     key_value = qkv[:, WIDTH:]
     picked23 = mm(pick23, key_value)
     small = by_head([picked23[8 * h : 8 * h + 8] for h in range(HEADS)])
-    s1[0] = jnp.concatenate([small, jnp.zeros_like(small)], 0).astype(BF)
-    s1_copies = [
-        push(s1.at[0], s1.at[d], s1_s.at[d], s1_r.at[d], group_peer[d]) for d in range(1, 16)
-    ]
+    sv[0] = small[:, :WIDTH]
+    sv[1] = small[:, WIDTH:]
+    sv_copy = push(sv.at[1 - core], sv_in, sib_s.at[0], sib_r.at[0], sibling)
     picked1 = mm(pick1, key_value)
     kv1[0] = by_head([picked1[64 * h : 64 * h + 64] for h in range(HEADS)]).astype(BF)
+    first = core == 0
+    sv_copy.wait_recv()
+    mine, theirs = sv[core], sv_in[...]
+    kvz[0] = jnp.concatenate(
+        [jnp.where(first, mine, theirs), jnp.where(first, theirs, mine)], 0
+    ).astype(BF)
+    kz_copies = [
+        push(kvz.at[0], kvz.at[d], kz_s.at[d], kz_r.at[d], z_peer[d]) for d in range(1, 8)
+    ]
     k1_copies = [
-        push(kv1.at[0], kv1.at[d], k1_s.at[d], k1_r.at[d], group_peer[d]) for d in range(1, 4)
+        push(kv1.at[0], kv1.at[d], k1_s.at[d], k1_r.at[d], pair_peer[d]) for d in range(1, 4)
     ]
-    sib_tok_copy = push(tok.at[1 - core], sib_tok, sib_s.at[0], sib_r.at[0], sibling)
+    sib_tok_copy = push(tok.at[1 - core], sib_tok, sib_s.at[1], sib_r.at[1], sibling)
 
     q_block1 = jnp.where(own1, mm(pick1, qkv[:, :WIDTH]), 0.0).astype(BF)
     q_block23 = jnp.where(own23, mm(pick23, qkv[:, :WIDTH]), 0.0).astype(BF)
@@ -224,20 +233,27 @@
     level0_forward(0)
 
     loads[4].wait()
-    for copy in s1_copies:
+    for copy in kz_copies:
         copy.wait_recv()
-    kv23[0] = mm(comp[...], s1[...].reshape(256, 2 * WIDTH)).astype(BF)
-    kz_copies = [
-        push(kv23.at[0], kv23.at[d], kz_s.at[d], kz_r.at[d], z_peer[d]) for d in range(1, 8)
-    ]
+    kvh[core, 0:80] = mm(comp[...], kvz[...].reshape(128, WIDTH)).astype(BF)
+    kx_copies = []
+    for d in range(1, 8):
+        if d < 4:
+            src, dst = kvh.at[core, 0:80], kvh.at[core, 80 * d : 80 * d + 80]
+        else:
+            src, dst = kvh.at[core, 64:80], kvh.at[core, 256 + 16 * d : 272 + 16 * d]
+        kx_copies.append(push(src, dst, kx_s.at[d], kx_r.at[d], chip_peer[d]))
 
     level0_forward(1)
+    for copy in kx_copies:
+        copy.wait_recv()
+    kvh_copy = push(kvh.at[core], kvh.at[core], sib_s.at[2], sib_r.at[2], sibling)
     level0_forward(2)
 
     loads[2].wait()
     loads[3].wait()
     gout_copy.wait_recv()
-    sib_gout_copy = push(gout.at[1 - core], sib_gout, sib_s.at[1], sib_r.at[1], sibling)
+    sib_gout_copy = push(gout.at[1 - core], sib_gout, sib_s.at[3], sib_r.at[3], sibling)
     grad_att = (mm(gout[0], wout[:, :HALF], NT) + mm(gout[1], wout[:, HALF:], NT)).astype(BF)
     gatt[...] = grad_att
     g_block1 = jnp.where(own1, mm(pick1, grad_att), 0.0).astype(BF)
@@ -253,16 +269,18 @@
     den_ref[...] += placed[:, WIDTH:]
 
     loads[5].wait()
+    sib_gout_copy.wait_recv()
+    gout_t[:, :ROWS] = mm(perm[...], gout[core], NT).astype(BF)
+    gout_t[:, ROWS:] = mm(perm[...], sib_gout[...], NT).astype(BF)
     sib_tok_copy.wait_recv()
     tok_t[:, :ROWS] = mm(perm[...], tok[core], NT).astype(BF)
     tok_t[:, ROWS:] = mm(perm[...], sib_tok[...], NT).astype(BF)
 
-    for copy in kz_copies:
-        copy.wait_recv()
-    keys23 = kv23[:, :, :WIDTH].reshape(WIDTH, WIDTH)
-    values23 = kv23[:, :, WIDTH:].reshape(WIDTH, WIDTH)
+    kvh_copy.wait_recv()
+    keys23, values23 = kvh[0], kvh[1]
     small_row = lax.rem(iota((8 * HEADS, WIDTH), 0), 8)
-    wide_key = lax.rem(iota((8 * HEADS, WIDTH), 1), 48) >= 32
+    key_at = iota((8 * HEADS, WIDTH), 1)
+    wide_key = (key_at >= 320) | (lax.rem(key_at, 80) >= 64)
     mask23 = jnp.where(wide_key, small_row, small_row + 8)
     mask23 = (mask23 == 4) | ((mask23 >= 8) & (mask23 < 12))
     weights, both = level_forward(q_block23, keys23, values23, own23, mask23)
@@ -272,7 +290,7 @@
     den = den_ref[...] + placed[:, WIDTH:]
     attended = (numer / den).astype(BF)
     att_buf[0] = attended
-    att_copy = push(att_buf.at[0], att_buf.at[1], sib_s.at[2], sib_r.at[2], sibling)
+    att_copy = push(att_buf.at[0], att_buf.at[1], sib_s.at[4], sib_r.at[4], sibling)
 
     inverse = 1.0 / den
     products = grad_att.astype(F32) * attended.astype(F32)
@@ -302,21 +320,54 @@
     grad_q23, grad_kv = level_backward(
         w23[...], q_block23, g_block23, keys23, values23, inv, delta, own23
     )
-    gsendz[...] = grad_kv.astype(BF).reshape(8, 48, 2 * WIDTH)
-    rz_copies = [
-        push(gsendz.at[d], grecvz.at[d], rz_s.at[d], rz_r.at[d], z_peer[d]) for d in range(1, 8)
-    ]
-
+    grad_kv = grad_kv.astype(BF)
+    gs[0] = grad_kv[:, :WIDTH]
+    gs[1] = grad_kv[:, WIDTH:]
+    gs_copy = push(gs.at[1 - core], gs_in, sib_s.at[5], sib_r.at[5], sibling)
+
+    def out_cols(which):
+        return pl.ds(pl.multiple_of(which * HALF, HALF), HALF)
+
+    mixed_out[...] = mm(attended, wout[:, out_cols(other_head)]).astype(BF)
+    mixed_copy = push(mixed_out, mixed_in, head_s.at[3], head_r.at[3], seq, other_head)
     inv, delta = picked_stats(pick1, 64)
     grad_q1, grad_kv = level_backward(
         w1[...], q_block1, g_block1, keys1, values1, inv, delta, own1
     )
     gsend1[...] = grad_kv.astype(BF).reshape(4, 64, 2 * WIDTH)
     r1_copies = [
-        push(gsend1.at[d], grecv1.at[d], r1_s.at[d], r1_r.at[d], group_peer[d])
+        push(gsend1.at[d], grecv1.at[d], r1_s.at[d], r1_r.at[d], pair_peer[d])
         for d in range(1, 4)
     ]
+    gs_copy.wait_recv()
+    gx[...] = (gs[core].astype(F32) + gs_in[...].astype(F32)).astype(BF)
+
+    def back_rows(d):
+        return slice(80 * d, 80 * d + 80) if d < 4 else slice(256 + 16 * d, 272 + 16 * d)
+
+    rx_copies = [
+        push(gx.at[back_rows(d)], gx_in.at[back_rows(d)], rx_s.at[d], rx_r.at[d], chip_peer[d])
+        for d in range(1, 8)
+    ]
     gq_acc[...] = place(put1, grad_q1) + place(put23, grad_q23)
+
+    def weight_term(left, own, other, arrived):
+        term = mm(left[:, :ROWS], own)
+        arrived.wait_recv()
+        return term + mm(left[:, ROWS:], other[...])
+
+    def y_block(d):
+        return lax.rem(lax.div(chip_peer[d], 2), 4)
+
+    def y_send(n, source, landing):
+        return [
+            push(source.at[y_block(d)], landing.at[d], y_s.at[n, d], y_r.at[n, d], chip_peer[d])
+            for d in range(1, 4)
+        ]
+
+    term = weight_term(gout_t, att_buf[0], att_buf.at[1], att_copy)
+    ysend[0] = term.astype(BF).reshape(4, 192, WIDTH)
+    yw = y_send(0, ysend.at[0], yrecv.at[0])
 
     def level0_backward(p):
         queries, keys, values = pair(0, p), pair(WIDTH, p), pair(2 * WIDTH, p)
@@ -339,73 +390,41 @@
         gkv_acc[:, WIDTH + 128 * p : WIDTH + 128 * p + 128] = merged[2]
 
     level0_backward(0)
+    for copy in rx_copies:
+        copy.wait_recv()
+    total = gx[0:80].astype(F32)
+    for d in range(1, 4):
+        total = total + gx_in[back_rows(d)].astype(F32)
+    wide = total[64:80]
+    for d in range(4, 8):
+        wide = wide + gx_in[back_rows(d)].astype(F32)
+    total = jnp.concatenate([total[:64], wide], 0).astype(BF)
+    gz[...] = mm(comp[...], total, TN).astype(BF).reshape(8, 16, WIDTH)
+    rz_copies = [
+        push(gz.at[d], gz_in.at[d], rz_s.at[d], rz_r.at[d], z_peer[d]) for d in range(1, 8)
+    ]
     level0_backward(1)
-
-    total = gsendz[0].astype(F32)
-    for d in range(1, 8):
-        rz_copies[d - 1].wait_recv()
-        total = total + grecvz[d].astype(F32)
-    gsends[...] = mm(comp[...], total.astype(BF), TN).astype(BF).reshape(16, 16, 2 * WIDTH)
-    rs_copies = [
-        push(gsends.at[d], grecvs.at[d], rs_s.at[d], rs_r.at[d], group_peer[d])
-        for d in range(1, 16)
-    ]
-
     level0_backward(2)
+    part_a[...] = mm(attended, wout[:, out_cols(head)])
     grad_q = gq_acc[...].astype(BF)
     gbuf[0, 0] = grad_q
-    gq_copy = push(gbuf.at[0, 0], gbuf.at[0, 1], sib_s.at[3], sib_r.at[3], sibling)
-
-    sib_gout_copy.wait_recv()
-    gout_t[:, :ROWS] = mm(perm[...], gout[core], NT).astype(BF)
-    gout_t[:, ROWS:] = mm(perm[...], sib_gout[...], NT).astype(BF)
-
-    def weight_terms(r, p, left, own, other):
-        term = mm(left[:, :ROWS], own) + mm(left[:, ROWS:], other)
-        ysend[r, :, p] = term.astype(BF).reshape(4, 192, WIDTH)
-
-    def y_stage(r):
-        copies = []
-        for d in range(1, 4):
-            block = lax.rem(lax.div(y_peer[d], 2), 4)
-            copies.append(push(
-                ysend.at[r, block], yrecv.at[r, d], y_s.at[r, d], y_r.at[r, d], y_peer[d]
-            ))
-        return copies
-
-    def z_stage(r, copies):
-        for copy in copies:
-            copy.wait_recv()
-        total = ysend[r, y_at].astype(F32)
-        for d in range(1, 4):
-            total = total + yrecv[r, d].astype(F32)
-        for n in range(8):
-            rows = slice(24 * n, 24 * n + 24)
-            zsend[r, n] = jnp.concatenate([total[0, rows], total[1, rows]], 0).astype(BF)
-        out = []
-        for d in range(1, 8):
-            block = lax.rem(lax.div(z_peer[d], 8), 8)
-            out.append(push(
-                zsend.at[r, block], zrecv.at[r, d], z_s.at[r, d], z_r.at[r, d], z_peer[d]
-            ))
-        return out
-
-    def x_stage(r, copies):
-        total = zsend[r, z_at].astype(F32)
-        for d in range(1, 8):
-            copies[d - 1].wait_recv()
-            total = total + zrecv[r, d].astype(F32)
-        xbuf[r] = total
-        out = []
-        for n, d in enumerate((1, 8, 9)):
-            out.append(push(xbuf.at[r], xrecv.at[r, n], x_s.at[r, n], x_r.at[r, n], group_peer[d]))
-        return out
-
-    att_copy.wait_recv()
-    weight_terms(0, 0, gout_t, att_buf[0], att_buf[1])
-    gq_copy.wait_recv()
-    weight_terms(0, 1, tok_t, gbuf[0, 0], gbuf[0, 1])
-    y0 = y_stage(0)
+    gq_copy = push(gbuf.at[0, 0], gbuf.at[0, 1], sib_s.at[6], sib_r.at[6], sibling)
+
+    for copy in rz_copies:
+        copy.wait_recv()
+    total = gz[0].astype(F32)
+    for d in range(1, 8):
+        total = total + gz_in[d].astype(F32)
+    gf[0] = total[:8]
+    gf[1] = total[8:]
+    gf_copy = push(gf.at[1 - core], gf_in, sib_s.at[7], sib_r.at[7], sibling)
+
+    term = weight_term(tok_t, grad_q, gbuf.at[0, 1], gq_copy)
+    ysend[1] = term.astype(BF).reshape(4, 192, WIDTH)
+    yq = y_send(1, ysend.at[1], yrecv.at[1])
+
+    def head_rows(which):
+        return pl.ds(pl.multiple_of(which * HALF, HALF), HALF)
 
     def tiled(x):
         return jnp.concatenate([x] * HEADS, 0)
@@ -416,67 +435,116 @@
         total = total + grecv1[d].astype(F32)
     both1 = jnp.concatenate([own1, own1], 1)
     grad_kv = gkv_acc[...] + place(put1, jnp.where(both1, tiled(total), 0.0))
-    total = gsends[0].astype(F32)
-    for d in range(1, 16):
-        rs_copies[d - 1].wait_recv()
-        total = total + grecvs[d].astype(F32)
+    gf_copy.wait_recv()
+    mine, theirs = gf[core], gf_in[...]
+    total = jnp.concatenate([jnp.where(first, mine, theirs), jnp.where(first, theirs, mine)], 1)
     both23 = jnp.concatenate([own23, own23], 1)
-    grad_kv = grad_kv + place(put23, jnp.where(both23, tiled(total[:8]), 0.0))
+    grad_kv = grad_kv + place(put23, jnp.where(both23, tiled(total), 0.0))
     grad_kv = grad_kv.astype(BF)
     gbuf[1, 0] = grad_kv[:, :WIDTH]
     gbuf[2, 0] = grad_kv[:, WIDTH:]
-    gk_copy = push(gbuf.at[1, 0], gbuf.at[1, 1], sib_s.at[4], sib_r.at[4], sibling)
-    gv_copy = push(gbuf.at[2, 0], gbuf.at[2, 1], sib_s.at[5], sib_r.at[5], sibling)
-
-    gk_copy.wait_recv()
-    weight_terms(1, 0, tok_t, gbuf[1, 0], gbuf[1, 1])
-    gv_copy.wait_recv()
-    weight_terms(1, 1, tok_t, gbuf[2, 0], gbuf[2, 1])
-    y1 = y_stage(1)
+    gk_copy = push(gbuf.at[1, 0], gbuf.at[1, 1], sib_s.at[8], sib_r.at[8], sibling)
+    gv_copy = push(gbuf.at[2, 0], gbuf.at[2, 1], sib_s.at[9], sib_r.at[9], sibling)
+
+    term_k = weight_term(tok_t, gbuf[1, 0], gbuf.at[1, 1], gk_copy).astype(BF)
+    term_v = weight_term(tok_t, gbuf[2, 0], gbuf.at[2, 1], gv_copy).astype(BF)
+    ysend_a[:, 0] = term_k[:, :256].reshape(4, 192, 256)
+    ysend_a[:, 1] = term_v[:, :256].reshape(4, 192, 256)
+    ya = y_send(2, ysend_a, yrecv_a)
+    ysend_b[:, 0] = term_k[:, 256:].reshape(4, 192, 128)
+    ysend_b[:, 1] = term_v[:, 256:].reshape(4, 192, 128)
+    yb = y_send(3, ysend_b, yrecv_b)
 
     def token_part(which):
-        rows = pl.ds(pl.multiple_of(which * HALF, HALF), HALF)
-        out = mm(gbuf[0, 0], wqkv[0, rows, :], NT)
-        out = out + mm(gbuf[1, 0], wqkv[1, rows, :], NT)
-        return out + mm(gbuf[2, 0], wqkv[2, rows, :], NT)
-
-    def mixed_part(which):
-        return mm(att_buf[0], wout[:, pl.ds(pl.multiple_of(which * HALF, HALF), HALF)])
+        out = mm(gbuf[0, 0], wqkv[0, head_rows(which), :], NT)
+        out = out + mm(gbuf[1, 0], wqkv[1, head_rows(which), :], NT)
+        return out + mm(gbuf[2, 0], wqkv[2, head_rows(which), :], NT)
 
     gtok_out[...] = token_part(other_head).astype(BF)
     gtok_copy = push(gtok_out, gtok_in, head_s.at[2], head_r.at[2], seq, other_head)
-    z0 = z_stage(0, y0)
-    mixed_out[...] = mixed_part(other_head).astype(BF)
-    mixed_copy = push(mixed_out, mixed_in, head_s.at[3], head_r.at[3], seq, other_head)
+
+    def z_send(n, total, source, landing):
+        for m in range(8):
+            rows = slice(24 * m, 24 * m + 24)
+            source[m] = jnp.concatenate([total[0][rows], total[1][rows]], 0).astype(BF)
+        out = []
+        for d in range(1, 8):
+            block = lax.rem(lax.div(z_peer[d], 8), 8)
+            out.append(
+                push(source.at[block], landing.at[d], z_s.at[n, d], z_r.at[n, d], z_peer[d])
+            )
+        return out
+
+    def y_total(own, landing):
+        out = own.astype(F32)
+        for d in range(1, 4):
+            out = out + landing[d].astype(F32)
+        return out
+
+    def z_total(own, landing):
+        out = own.astype(F32)
+        for d in range(1, 8):
+            out = out + landing[d].astype(F32)
+        return out
+
+    def arrive(copies):
+        for copy in copies:
+            copy.wait_recv()
+
+    def x_send(r):
+        return [
+            push(xbuf.at[r], xrecv.at[r, d], x_s.at[r, d], x_r.at[r, d], cross_peer[d])
+            for d in range(1, 4)
+        ]
+
+    arrive(yw)
+    arrive(yq)
+    totals = [y_total(ysend[p, y_at], yrecv.at[p]) for p in range(2)]
+    z0 = z_send(0, totals, zsend, zrecv)
+    arrive(ya)
+    za = z_send(1, y_total(ysend_a[y_at], yrecv_a), zsend_a, zrecv_a)
+    arrive(yb)
+    zb = z_send(2, y_total(ysend_b[y_at], yrecv_b), zsend_b, zrecv_b)
+    arrive(z0)
+    xbuf[0] = z_total(zsend[z_at], zrecv)
+    x0 = x_send(0)
     own_tokens = token_part(head)
-    z1 = z_stage(1, y1)
-    x0 = x_stage(0, z0)
     gtok_copy.wait_recv()
     gtok_ref[...] = (own_tokens + gtok_in[...].astype(F32)).astype(BF)
-    own_mixed = mixed_part(head)
     mixed_copy.wait_recv()
-    mixed_ref[...] = (own_mixed + mixed_in[...].astype(F32)).astype(BF)
-    x1 = x_stage(1, z1)
+    mixed_ref[...] = (part_a[...] + mixed_in[...].astype(F32)).astype(BF)
+    arrive(za)
+    xbuf[1, :, :256] = z_total(zsend_a[z_at], zrecv_a)
+    arrive(zb)
+    xbuf[1, :, 256:] = z_total(zsend_b[z_at], zrecv_b)
+    x1 = x_send(1)
 
     def finish(r, copies):
-        for copy in copies:
-            copy.wait_recv()
-        straight = xbuf[r] + xrecv[r, 1]
-        crossed = xrecv[r, 0] + xrecv[r, 2]
+        arrive(copies)
+        straight = xbuf[r] + xrecv[r, 2]
+        crossed = xrecv[r, 1] + xrecv[r, 3]
         total = jnp.where(core == x_at, straight, crossed)
         return [
-            jnp.where(core == 0, total[24 * n : 24 * n + 12], total[24 * n + 12 : 24 * n + 24])
+            jnp.where(first, total[24 * n : 24 * n + 12], total[24 * n + 12 : 24 * n + 24])
             for n in range(2)
         ]
 
-    first, second = finish(0, x0)
-    gwout_ref[...] = first
-    gqkv_ref[0] = second
-    first, second = finish(1, x1)
-    gqkv_ref[1] = first
-    gqkv_ref[2] = second
+    one, two = finish(0, x0)
+    gwout_ref[...] = one
+    gqkv_ref[0] = two
+    one, two = finish(1, x1)
+    gqkv_ref[1] = one
+    gqkv_ref[2] = two
     for copy in sent:
         copy.wait_send()
+
+
+def finish_kernel(mixed, gtok, gqkv, gwout, mixed_out, gtok_out, gqkv_out, gwout_out):
+    mixed_out[...] = mixed[...]
+    gtok_out[...] = gtok[...]
+    gwout_out[...] = gwout[...]
+    for j in range(3):
+        gqkv_out[:, j, :] = gqkv[j]
 
 
 def constants():
@@ -484,11 +552,12 @@
     y, z, i = at // 192, at % 192 // 24, at % 24
     perm = np.zeros((HALF, HALF), np.float32)
     perm[at, z * 96 + y * 24 + i] = 1
-    comp = np.zeros((48, 256), np.float32)
-    for r in range(32):
-        comp[r, r // 4 * 16 + r % 4] = 1
-    for d in range(16):
-        comp[32 + d, 16 * d + 4] = 1
+    comp = np.zeros((80, 128), np.float32)
+    for d in range(8):
+        for e in range(2):
+            for i in range(4):
+                comp[8 * d + 4 * e + i, 16 * d + 8 * e + i] = 1
+            comp[64 + 2 * d + e, 16 * d + 8 * e + 4] = 1
     return jnp.asarray(perm, BF), jnp.asarray(comp, BF)
 
 
@@ -498,29 +567,36 @@
     dma = pltpu.SemaphoreType.DMA
     scratch = [
         vm((2, ROWS, HALF), BF), vm((2, ROWS, HALF), BF), vm((3, 2 * HALF, WIDTH), BF),
-        vm((WIDTH, 2 * HALF), BF), vm((HALF, HALF), BF), vm((48, 256), BF),
+        vm((WIDTH, 2 * HALF), BF), vm((HALF, HALF), BF), vm((80, 128), BF),
         vm((ROWS, HALF), BF), vm((ROWS, HALF), BF),
-        vm((ROWS, 3 * WIDTH), F32), vm((ROWS, 3 * WIDTH), BF),
-        vm((4, 64, 2 * WIDTH), BF), vm((16, 16, 2 * WIDTH), BF), vm((8, 48, 2 * WIDTH), BF),
+        vm((ROWS, 3 * WIDTH), F32), vm((ROWS, 3 * WIDTH), BF), vm((4, 64, 2 * WIDTH), BF),
+        vm((2, 8, WIDTH), F32), vm((8, WIDTH), F32), vm((8, 16, WIDTH), BF),
+        vm((2, WIDTH, WIDTH), BF),
         vm((HEADS, ROWS, ROWS), F32), vm((WIDTH, ROWS), F32), vm((8 * HEADS, WIDTH), F32),
         vm((ROWS, WIDTH), F32), vm((ROWS, WIDTH), F32), vm((ROWS, WIDTH), BF),
         vm((2, ROWS, WIDTH), BF), vm((ROWS, WIDTH), F32), vm((ROWS, 2 * WIDTH), F32),
         vm((HALF, 2 * ROWS), BF), vm((HALF, 2 * ROWS), BF), vm((3, 2, ROWS, WIDTH), BF),
         vm((4, 64, 2 * WIDTH), BF), vm((4, 64, 2 * WIDTH), BF),
-        vm((8, 48, 2 * WIDTH), BF), vm((8, 48, 2 * WIDTH), BF),
-        vm((16, 16, 2 * WIDTH), BF), vm((16, 16, 2 * WIDTH), BF),
+        vm((2, WIDTH, WIDTH), BF), vm((WIDTH, WIDTH), BF),
+        vm((WIDTH, WIDTH), BF), vm((WIDTH, WIDTH), BF),
+        vm((8, 16, WIDTH), BF), vm((8, 16, WIDTH), BF),
+        vm((2, 8, WIDTH), F32), vm((8, WIDTH), F32),
         vm((ROWS, HALF), BF), vm((ROWS, HALF), BF), vm((ROWS, HALF), BF), vm((ROWS, HALF), BF),
-        vm((2, 4, 2, 192, WIDTH), BF), vm((2, 4, 2, 192, WIDTH), BF),
-        vm((2, 8, 48, WIDTH), BF), vm((2, 8, 48, WIDTH), BF),
-        vm((2, 48, WIDTH), F32), vm((2, 3, 48, WIDTH), F32),
-        dma((6,)), dma((4,)), dma((4,)), dma((6,)), dma((6,)), dma((4,)), dma((4,)),
-        dma((16,)), dma((16,)), dma((8,)), dma((8,)), dma((4,)), dma((4,)), dma((8,)), dma((8,)),
-        dma((16,)), dma((16,)), dma((2, 4)), dma((2, 4)), dma((2, 8)), dma((2, 8)),
-        dma((2, 3)), dma((2, 3)),
+        vm((ROWS, HALF), F32),
+        vm((2, 4, 192, WIDTH), BF), vm((2, 4, 192, WIDTH), BF),
+        vm((4, 2, 192, 256), BF), vm((4, 2, 192, 256), BF),
+        vm((4, 2, 192, 128), BF), vm((4, 2, 192, 128), BF),
+        vm((8, 48, WIDTH), BF), vm((8, 48, WIDTH), BF),
+        vm((8, 48, 256), BF), vm((8, 48, 256), BF), vm((8, 48, 128), BF), vm((8, 48, 128), BF),
+        vm((2, 48, WIDTH), F32), vm((2, 4, 48, WIDTH), F32),
+        dma((6,)), dma((4,)), dma((4,)), dma((10,)), dma((10,)), dma((4,)), dma((4,)),
+        dma((8,)), dma((8,)), dma((8,)), dma((8,)), dma((4,)), dma((4,)),
+        dma((8,)), dma((8,)), dma((8,)), dma((8,)), dma((4, 4)), dma((4, 4)),
+        dma((3, 8)), dma((3, 8)), dma((2, 4)), dma((2, 4)),
     ]
     anywhere = pl.BlockSpec(memory_space=pl.ANY)
     inside = pl.BlockSpec(memory_space=pltpu.VMEM)
-    mixed, grad_tokens, grad_qkv, grad_w_out = pl.pallas_call(
+    results = pl.pallas_call(
         kernel,
         out_shape=(
             jax.ShapeDtypeStruct((ROWS, HALF), BF),
@@ -538,7 +614,18 @@
             flops=8 * 10**9, bytes_accessed=12 * 2**20, transcendentals=600000
         ),
     )(tokens, grad_out, jnp.transpose(w_qkv, (1, 0, 2)), w_out, perm, comp, offsets)
-    return mixed, grad_tokens, jnp.transpose(grad_qkv, (1, 0, 2)), jnp.transpose(grad_w_out)
+    mixed, grad_tokens, grad_qkv, grad_w_out = pl.pallas_call(
+        finish_kernel,
+        out_shape=(
+            jax.ShapeDtypeStruct((ROWS, HALF), BF),
+            jax.ShapeDtypeStruct((ROWS, HALF), BF),
+            jax.ShapeDtypeStruct((12, 3, WIDTH), F32),
+            jax.ShapeDtypeStruct((12, WIDTH), F32),
+        ),
+        in_specs=[inside] * 4,
+        out_specs=(inside,) * 4,
+    )(*results)
+    return mixed, grad_tokens, grad_qkv, jnp.transpose(grad_w_out)
 
 
 def solution(mesh):

time: 125 us -> 97.4 us (0.78)
  Pallas kernels: 120 us -> 96.7 us
  local copies, waits for them, and re-layouts: 4.72 us -> 0 us
    pallas_call x1, Pallas kernels: 120 us -> 94.6 us  [per_device(): pl.pallas_call(kernel, out_shape=(jax.ShapeDtypeStruct((ROWS, HALF), BF),...]
    unnamed x8 -> x0, local copies, waits for them, and re-layouts: 4.72 us -> none
    pallas_call x0 -> x1, Pallas kernels: none -> 2.05 us  [per_device(): pl.pallas_call(finish_kernel, out_shape=(jax.ShapeDtypeStruct((ROWS, HALF...]
where the time goes in v2:
time: 97.4 us; the launch traced here: 97.3 us
  Pallas kernels  96.7 us (99%)
    pallas_call x1, Pallas kernels, per_device(): pl.pallas_call(kernel, out_shape=(jax.ShapeDtypeStruct((ROWS, HALF), BF),...  94.6 us
    pallas_call x1, Pallas kernels, per_device(): pl.pallas_call(finish_kernel, out_shape=(jax.ShapeDtypeStruct((ROWS, HALF...  2.05 us

profile of v2, /device:TPU:1, one launch (start us, length us, event | category | flops | bytes accessed | tf_op | source)
XLA Modules:
  0.0 97.3 jit_solution(15272722864699808904)
XLA Ops:
  0.6 94.6 %shard_map.102 = (bf16[256,768]{1,0:T(8,128)(2,1)}, bf16[256,768]{1,0:T(8,128)(2,1)}, f32[3,12,384]{2,1,0:T(8,128)}, f32[12,384]{1,0:T(8,128)}) custom-call(bf16[256,768]{1,0:T(8,128)(2,1)} %tok_hbm.1, bf16[256,768]{1,0:T(8,128)(2,1)} %gout_hbm.1, bf16[3,1536,384]{2,1,0:T(8,128)(2,1)} %bitcast.2, bf16[384,1536]{1,0:T(8,128)(2,1)} %wout_hbm.1, ...), custom_call_target="tpu_custom_call" | custom-call | flops 8000000000 | bytes 12582912 | tf_op jit(solution)/shard_map/pallas_call | solution.py:599
  95.2 2.1 %shard_map.103 = (bf16[256,768]{1,0:T(8,128)(2,1)}, bf16[256,768]{1,0:T(8,128)(2,1)}, f32[12,3,384]{2,1,0:T(4,128)}, f32[12,384]{1,0:T(8,128)}) custom-call(bf16[256,768]{1,0:T(8,128)(2,1)} %get-tuple-element.12.mixed, bf16[256,768]{1,0:T(8,128)(2,1)} %get-tuple-element.13.gtok, f32[3,12,384]{2,1,0:T(8,128)} %get-tuple-element.14.gqkv, ...), custom_call_target="tpu_custom_call" | custom-call | tf_op jit(solution)/shard_map/pallas_call | solution.py:617

commit v3 on v2

--- a/solution.py
+++ b/solution.py
@@ -14,6 +14,7 @@
 HALF = 768
 HEADS = 6
 SCALE = 0.125
+FAR_FIRST = (4, 5, 3, 6, 2, 7, 1)
 
 NN = (((1,), (0,)), ((), ()))
 NT = (((1,), (1,)), ((), ()))
@@ -81,11 +82,11 @@
     tok, gout, wqkv, wout, perm, comp, sib_tok, sib_gout,
     acc, qkv, kv1, sv, sv_in, kvz, kvh, w0, w1, w23, numer_ref, den_ref, gatt, att_buf,
     gq_acc, gkv_acc, tok_t, gout_t, gbuf, gsend1, grecv1, gs, gs_in, gx, gx_in, gz, gz_in,
-    gf, gf_in, mixed_out, mixed_in, gtok_out, gtok_in, part_a,
+    gf, gf_in, picks, rows_out, rows_in, xin, fbuf, mixed_out, mixed_in, gtok_out, gtok_in, part_a,
     ysend, yrecv, ysend_a, yrecv_a, ysend_b, yrecv_b, zsend, zrecv, zsend_a, zrecv_a,
     zsend_b, zrecv_b, xbuf, xrecv,
     local_sem, head_s, head_r, sib_s, sib_r, k1_s, k1_r, kz_s, kz_r, kx_s, kx_r,
-    r1_s, r1_r, rx_s, rx_r, rz_s, rz_r, y_s, y_r, z_s, z_r, x_s, x_r,
+    r1_s, r1_r, rx_s, rx_r, rz_s, rz_r, y_s, y_r, z_s, z_r, x_s, x_r, w_s, w_r,
 ):
     seq = lax.axis_index("seq")
     head = lax.axis_index("head")
@@ -112,12 +113,15 @@
     sibling = pair_peer[1]
     other_head = 1 - head
 
-    def push(src, dst, send, recv, to_seq, to_head=None):
+    def made(src, dst, send, recv, to_seq, to_head=None):
         target = (to_seq, head if to_head is None else to_head)
-        copy = pltpu.make_async_remote_copy(
+        return pltpu.make_async_remote_copy(
             src_ref=src, dst_ref=dst, send_sem=send, recv_sem=recv,
             device_id=target, device_id_type=MESH,
         )
+
+    def push(*copy_args):
+        copy = made(*copy_args)
         copy.start()
         sent.append(copy)
         return copy
@@ -132,23 +136,6 @@
         copy = pltpu.make_async_copy(src, dst, local_sem.at[n])
         copy.start()
         loads.append(copy)
-
-    barrier = pltpu.get_barrier_semaphore()
-    peers = [(seq, other_head)]
-    peers += [(sibling, head), (pair_peer[3], head), (cross_peer[3], head)]
-    peers += [(chip_peer[d], head) for d in range(1, 8)]
-    peers += [(z_peer[d], head) for d in range(1, 8)]
-    for peer in peers:
-        pl.semaphore_signal(barrier, inc=1, device_id=peer, device_id_type=MESH)
-    pl.semaphore_wait(barrier, len(peers))
-
-    tok_copy = push(tok_hbm, tok.at[head], head_s.at[0], head_r.at[0], seq, other_head)
-
-    loads[0].wait()
-    loads[1].wait()
-    for j in range(3):
-        cols = slice(WIDTH * j, WIDTH * (j + 1))
-        acc[:, cols] = mm(tok[head], wqkv[j, pl.ds(pl.multiple_of(head * HALF, HALF), HALF), :])
 
     lane = iota((64, ROWS), 1)
     row = iota((64, ROWS), 0)
@@ -179,8 +166,72 @@
     own1 = block_mask(64)
     own23 = block_mask(8)
 
+    picks[0] = pick23
+    barrier = pltpu.get_barrier_semaphore()
+    peers = [(seq, other_head)]
+    peers += [(sibling, head), (pair_peer[3], head), (cross_peer[3], head)]
+    peers += [(chip_peer[d], head) for d in range(1, 8)]
+    peers += [(z_peer[d], head) for d in range(1, 8)]
+    for peer in peers:
+        pl.semaphore_signal(barrier, inc=1, device_id=peer, device_id_type=MESH)
+    pl.semaphore_wait(barrier, len(peers))
+
+    picks_copy = push(picks.at[0], picks.at[1], head_s.at[4], head_r.at[4], seq, other_head)
+
+    loads[0].wait()
+    chosen_own = mm(pick23, tok[head]).astype(BF)
+    picks_copy.wait_recv()
+    rows_out[...] = mm(picks[1], tok[head]).astype(BF)
+    rows_copy = push(rows_out, rows_in, head_s.at[5], head_r.at[5], seq, other_head)
+    tok_copy = push(tok_hbm, tok.at[head], head_s.at[0], head_r.at[0], seq, other_head)
+
+    def gout_push(n, rows):
+        return push(
+            gout_hbm.at[rows], gout.at[head, rows], head_s.at[n], head_r.at[n], seq, other_head
+        )
+
+    gout_copies = [gout_push(1, slice(0, 112))]
+    loads[1].wait()
+
+    def head_rows(which):
+        return pl.ds(pl.multiple_of(which * HALF, HALF), HALF)
+
+    small_own = [mm(chosen_own, wqkv[j, head_rows(head), :]) for j in (1, 2)]
+    rows_copy.wait_recv()
+    chosen_other = rows_in[...]
+    for j in (1, 2):
+        part = small_own[j - 1] + mm(chosen_other, wqkv[j, head_rows(other_head), :])
+        part = by_head([part[8 * h : 8 * h + 8] for h in range(HEADS)])
+        sv[j - 1] = part.astype(BF).astype(F32)
+    sv_copy = push(sv.at[1 - core], sv_in, sib_s.at[0], sib_r.at[0], sibling)
+
+    for j in range(3):
+        cols = slice(WIDTH * j, WIDTH * (j + 1))
+        acc[:, cols] = mm(tok[head], wqkv[j, pl.ds(pl.multiple_of(head * HALF, HALF), HALF), :])
+
+    first = core == 0
+    sv_copy.wait_recv()
+    mine, theirs = sv[core], sv_in[...]
+    kvz[0] = jnp.concatenate(
+        [jnp.where(first, mine, theirs), jnp.where(first, theirs, mine)], 0
+    ).astype(BF)
+    kz_copies = [
+        push(kvz.at[0], kvz.at[d], kz_s.at[d], kz_r.at[d], z_peer[d]) for d in FAR_FIRST
+    ]
+    loads[4].wait()
+    for copy in kz_copies:
+        copy.wait_recv()
+    kvh[core, 0:80] = mm(comp[...], kvz[...].reshape(128, WIDTH)).astype(BF)
+    kx_copies = []
+    for d in (6, 5, 7, 4, 2, 1, 3):
+        if d < 4:
+            src, dst = kvh.at[core, 0:80], kvh.at[core, 80 * d : 80 * d + 80]
+        else:
+            src, dst = kvh.at[core, 64:80], kvh.at[core, 256 + 16 * d : 272 + 16 * d]
+        kx_copies.append(push(src, dst, kx_s.at[d], kx_r.at[d], chip_peer[d]))
+    gout_copies.append(gout_push(6, slice(112, ROWS)))
+
     tok_copy.wait_recv()
-    gout_copy = push(gout_hbm, gout.at[head], head_s.at[1], head_r.at[1], seq, other_head)
     for j in range(3):
         cols = slice(WIDTH * j, WIDTH * (j + 1))
         other_rows = pl.ds(pl.multiple_of(other_head * HALF, HALF), HALF)
@@ -190,24 +241,10 @@
         qkv[:, cols] = part.astype(BF)
 
     key_value = qkv[:, WIDTH:]
-    picked23 = mm(pick23, key_value)
-    small = by_head([picked23[8 * h : 8 * h + 8] for h in range(HEADS)])
-    sv[0] = small[:, :WIDTH]
-    sv[1] = small[:, WIDTH:]
-    sv_copy = push(sv.at[1 - core], sv_in, sib_s.at[0], sib_r.at[0], sibling)
     picked1 = mm(pick1, key_value)
     kv1[0] = by_head([picked1[64 * h : 64 * h + 64] for h in range(HEADS)]).astype(BF)
-    first = core == 0
-    sv_copy.wait_recv()
-    mine, theirs = sv[core], sv_in[...]
-    kvz[0] = jnp.concatenate(
-        [jnp.where(first, mine, theirs), jnp.where(first, theirs, mine)], 0
-    ).astype(BF)
-    kz_copies = [
-        push(kvz.at[0], kvz.at[d], kz_s.at[d], kz_r.at[d], z_peer[d]) for d in range(1, 8)
-    ]
     k1_copies = [
-        push(kv1.at[0], kv1.at[d], k1_s.at[d], k1_r.at[d], pair_peer[d]) for d in range(1, 4)
+        push(kv1.at[0], kv1.at[d], k1_s.at[d], k1_r.at[d], pair_peer[d]) for d in range(1, 3)
     ]
     sib_tok_copy = push(tok.at[1 - core], sib_tok, sib_s.at[1], sib_r.at[1], sibling)
 
@@ -232,35 +269,16 @@
 
     level0_forward(0)
 
-    loads[4].wait()
-    for copy in kz_copies:
-        copy.wait_recv()
-    kvh[core, 0:80] = mm(comp[...], kvz[...].reshape(128, WIDTH)).astype(BF)
-    kx_copies = []
-    for d in range(1, 8):
-        if d < 4:
-            src, dst = kvh.at[core, 0:80], kvh.at[core, 80 * d : 80 * d + 80]
-        else:
-            src, dst = kvh.at[core, 64:80], kvh.at[core, 256 + 16 * d : 272 + 16 * d]
-        kx_copies.append(push(src, dst, kx_s.at[d], kx_r.at[d], chip_peer[d]))
-
     level0_forward(1)
     for copy in kx_copies:
         copy.wait_recv()
     kvh_copy = push(kvh.at[core], kvh.at[core], sib_s.at[2], sib_r.at[2], sibling)
     level0_forward(2)
 
-    loads[2].wait()
-    loads[3].wait()
-    gout_copy.wait_recv()
-    sib_gout_copy = push(gout.at[1 - core], sib_gout, sib_s.at[3], sib_r.at[3], sibling)
-    grad_att = (mm(gout[0], wout[:, :HALF], NT) + mm(gout[1], wout[:, HALF:], NT)).astype(BF)
-    gatt[...] = grad_att
-    g_block1 = jnp.where(own1, mm(pick1, grad_att), 0.0).astype(BF)
-    g_block23 = jnp.where(own23, mm(pick23, grad_att), 0.0).astype(BF)
-
-    for copy in k1_copies:
-        copy.wait_recv()
+    k1_copies[1].wait_recv()
+    k1_copies.append(push(kv1.at[2], kv1.at[3], k1_s.at[3], k1_r.at[3], sibling))
+    k1_copies[0].wait_recv()
+    k1_copies[2].wait_recv()
     keys1, values1 = kv1[:, :, :WIDTH].reshape(256, WIDTH), kv1[:, :, WIDTH:].reshape(256, WIDTH)
     weights, both = level_forward(q_block1, keys1, values1, own1, None)
     w1[...] = weights
@@ -269,12 +287,19 @@
     den_ref[...] += placed[:, WIDTH:]
 
     loads[5].wait()
-    sib_gout_copy.wait_recv()
-    gout_t[:, :ROWS] = mm(perm[...], gout[core], NT).astype(BF)
-    gout_t[:, ROWS:] = mm(perm[...], sib_gout[...], NT).astype(BF)
     sib_tok_copy.wait_recv()
     tok_t[:, :ROWS] = mm(perm[...], tok[core], NT).astype(BF)
     tok_t[:, ROWS:] = mm(perm[...], sib_tok[...], NT).astype(BF)
+
+    loads[2].wait()
+    loads[3].wait()
+    for copy in gout_copies:
+        copy.wait_recv()
+    sib_gout_copy = push(gout.at[1 - core], sib_gout, sib_s.at[3], sib_r.at[3], sibling)
+    grad_att = (mm(gout[0], wout[:, :HALF], NT) + mm(gout[1], wout[:, HALF:], NT)).astype(BF)
+    gatt[...] = grad_att
+    g_block1 = jnp.where(own1, mm(pick1, grad_att), 0.0).astype(BF)
+    g_block23 = jnp.where(own23, mm(pick23, grad_att), 0.0).astype(BF)
 
     kvh_copy.wait_recv()
     keys23, values23 = kvh[0], kvh[1]
@@ -328,47 +353,14 @@
     def out_cols(which):
         return pl.ds(pl.multiple_of(which * HALF, HALF), HALF)
 
-    mixed_out[...] = mm(attended, wout[:, out_cols(other_head)]).astype(BF)
-    mixed_copy = push(mixed_out, mixed_in, head_s.at[3], head_r.at[3], seq, other_head)
     inv, delta = picked_stats(pick1, 64)
     grad_q1, grad_kv = level_backward(
         w1[...], q_block1, g_block1, keys1, values1, inv, delta, own1
     )
     gsend1[...] = grad_kv.astype(BF).reshape(4, 64, 2 * WIDTH)
     r1_copies = [
-        push(gsend1.at[d], grecv1.at[d], r1_s.at[d], r1_r.at[d], pair_peer[d])
-        for d in range(1, 4)
+        push(gsend1.at[d], grecv1.at[d], r1_s.at[d], r1_r.at[d], sibling) for d in (1, 3)
     ]
-    gs_copy.wait_recv()
-    gx[...] = (gs[core].astype(F32) + gs_in[...].astype(F32)).astype(BF)
-
-    def back_rows(d):
-        return slice(80 * d, 80 * d + 80) if d < 4 else slice(256 + 16 * d, 272 + 16 * d)
-
-    rx_copies = [
-        push(gx.at[back_rows(d)], gx_in.at[back_rows(d)], rx_s.at[d], rx_r.at[d], chip_peer[d])
-        for d in range(1, 8)
-    ]
-    gq_acc[...] = place(put1, grad_q1) + place(put23, grad_q23)
-
-    def weight_term(left, own, other, arrived):
-        term = mm(left[:, :ROWS], own)
-        arrived.wait_recv()
-        return term + mm(left[:, ROWS:], other[...])
-
-    def y_block(d):
-        return lax.rem(lax.div(chip_peer[d], 2), 4)
-
-    def y_send(n, source, landing):
-        return [
-            push(source.at[y_block(d)], landing.at[d], y_s.at[n, d], y_r.at[n, d], chip_peer[d])
-            for d in range(1, 4)
-        ]
-
-    term = weight_term(gout_t, att_buf[0], att_buf.at[1], att_copy)
-    ysend[0] = term.astype(BF).reshape(4, 192, WIDTH)
-    yw = y_send(0, ysend.at[0], yrecv.at[0])
-
     def level0_backward(p):
         queries, keys, values = pair(0, p), pair(WIDTH, p), pair(2 * WIDTH, p)
         grads = gatt[:, 128 * p : 128 * p + 128]
@@ -389,7 +381,90 @@
         gkv_acc[:, cols] = merged[1]
         gkv_acc[:, WIDTH + 128 * p : WIDTH + 128 * p + 128] = merged[2]
 
+    gq_acc[...] = place(put1, grad_q1) + place(put23, grad_q23)
     level0_backward(0)
+    gs_copy.wait_recv()
+    gx[...] = (gs[core].astype(F32) + gs_in[...].astype(F32)).astype(BF)
+
+    def back_rows(d):
+        return slice(80 * d, 80 * d + 80) if d < 4 else slice(256 + 16 * d, 272 + 16 * d)
+
+    rx_copies = [
+        push(gx.at[back_rows(d)], gx_in.at[back_rows(d)], rx_s.at[d], rx_r.at[d], chip_peer[d])
+        for d in range(1, 8)
+    ]
+    def weight_term(left, own, other, arrived):
+        term = mm(left[:, :ROWS], own)
+        arrived.wait_recv()
+        return term + mm(left[:, ROWS:], other[...])
+
+    def y_block(d):
+        return lax.rem(lax.div(chip_peer[d], 2), 4)
+
+    def y_made(n, source, landing):
+        return [
+            made(source.at[y_block(d)], landing.at[d], y_s.at[n, d], y_r.at[n, d], chip_peer[d])
+            for d in range(1, 4)
+        ]
+
+    def begin(copies):
+        for copy in copies:
+            copy.start()
+
+    def y_send(n, source, landing):
+        copies = y_made(n, source, landing)
+        begin(copies)
+        sent.extend(copies)
+        return copies
+
+    def y_total(own, landing):
+        out = own.astype(F32)
+        for d in range(1, 4):
+            out = out + landing[d].astype(F32)
+        return out
+
+    def z_total(own, landing):
+        out = own.astype(F32)
+        for d in range(1, 8):
+            out = out + landing[d].astype(F32)
+        return out
+
+    def arrive(copies):
+        for copy in copies:
+            copy.wait_recv()
+
+    reducer = core == x_at
+    x_copies = [
+        made(ysend.at[n], xin.at[n], w_s.at[n], w_r.at[n], cross_peer[2]) for n in range(2)
+    ]
+    y_early = [y_made(n, ysend.at[n], yrecv.at[n]) for n in range(2)]
+
+    def x_first(n, term):
+        ysend[n] = term.astype(BF).reshape(4, 192, WIDTH)
+
+        @pl.when(jnp.logical_not(reducer))
+        def _():
+            x_copies[n].start()
+
+    def y_after_x(n):
+        @pl.when(reducer)
+        def _():
+            x_copies[n].wait_recv()
+            ysend[n] = (ysend[n].astype(F32) + xin[n].astype(F32)).astype(BF)
+            begin(y_early[n])
+
+    sib_gout_copy.wait_recv()
+    gout_t[:, :ROWS] = mm(perm[...], gout[core], NT).astype(BF)
+    gout_t[:, ROWS:] = mm(perm[...], sib_gout[...], NT).astype(BF)
+    x_first(0, weight_term(gout_t, att_buf[0], att_buf.at[1], att_copy))
+
+    level0_backward(1)
+    level0_backward(2)
+    part_a[...] = mm(attended, wout[:, out_cols(head)])
+    grad_q = gq_acc[...].astype(BF)
+    gbuf[0, 0] = grad_q
+    gq_copy = push(gbuf.at[0, 0], gbuf.at[0, 1], sib_s.at[6], sib_r.at[6], sibling)
+
     for copy in rx_copies:
         copy.wait_recv()
     total = gx[0:80].astype(F32)
@@ -401,15 +476,15 @@
     total = jnp.concatenate([total[:64], wide], 0).astype(BF)
     gz[...] = mm(comp[...], total, TN).astype(BF).reshape(8, 16, WIDTH)
     rz_copies = [
-        push(gz.at[d], gz_in.at[d], rz_s.at[d], rz_r.at[d], z_peer[d]) for d in range(1, 8)
+        push(gz.at[d], gz_in.at[d], rz_s.at[d], rz_r.at[d], z_peer[d]) for d in FAR_FIRST
     ]
-    level0_backward(1)
-    level0_backward(2)
-    part_a[...] = mm(attended, wout[:, out_cols(head)])
-    grad_q = gq_acc[...].astype(BF)
-    gbuf[0, 0] = grad_q
-    gq_copy = push(gbuf.at[0, 0], gbuf.at[0, 1], sib_s.at[6], sib_r.at[6], sibling)
-
+    x_first(1, weight_term(tok_t, grad_q, gbuf.at[0, 1], gq_copy))
+    mixed_out[...] = mm(attended, wout[:, out_cols(other_head)]).astype(BF)
+    mixed_copy = push(mixed_out, mixed_in, head_s.at[3], head_r.at[3], seq, other_head)
+    y_after_x(0)
+    arrive(r1_copies)
+    gsend1[2] = (gsend1[2].astype(F32) + grecv1[3].astype(F32)).astype(BF)
+    r1_copies.append(push(gsend1.at[2], grecv1.at[2], r1_s.at[2], r1_r.at[2], pair_peer[2]))
     for copy in rz_copies:
         copy.wait_recv()
     total = gz[0].astype(F32)
@@ -419,19 +494,12 @@
     gf[1] = total[8:]
     gf_copy = push(gf.at[1 - core], gf_in, sib_s.at[7], sib_r.at[7], sibling)
 
-    term = weight_term(tok_t, grad_q, gbuf.at[0, 1], gq_copy)
-    ysend[1] = term.astype(BF).reshape(4, 192, WIDTH)
-    yq = y_send(1, ysend.at[1], yrecv.at[1])
-
-    def head_rows(which):
-        return pl.ds(pl.multiple_of(which * HALF, HALF), HALF)
-
     def tiled(x):
         return jnp.concatenate([x] * HEADS, 0)
 
     total = gsend1[0].astype(F32)
-    for d in range(1, 4):
-        r1_copies[d - 1].wait_recv()
+    r1_copies[2].wait_recv()
+    for d in range(1, 3):
         total = total + grecv1[d].astype(F32)
     both1 = jnp.concatenate([own1, own1], 1)
     grad_kv = gkv_acc[...] + place(put1, jnp.where(both1, tiled(total), 0.0))
@@ -446,15 +514,34 @@
     gk_copy = push(gbuf.at[1, 0], gbuf.at[1, 1], sib_s.at[8], sib_r.at[8], sibling)
     gv_copy = push(gbuf.at[2, 0], gbuf.at[2, 1], sib_s.at[9], sib_r.at[9], sibling)
 
-    term_k = weight_term(tok_t, gbuf[1, 0], gbuf.at[1, 1], gk_copy).astype(BF)
-    term_v = weight_term(tok_t, gbuf[2, 0], gbuf.at[2, 1], gv_copy).astype(BF)
-    ysend_a[:, 0] = term_k[:, :256].reshape(4, 192, 256)
-    ysend_a[:, 1] = term_v[:, :256].reshape(4, 192, 256)
+    term_k = weight_term(tok_t, gbuf[1, 0], gbuf.at[1, 1], gk_copy)
+    term_v = weight_term(tok_t, gbuf[2, 0], gbuf.at[2, 1], gv_copy)
+    ysend_a[:, 0] = term_k[:, :256].astype(BF).reshape(4, 192, 256)
+    ysend_a[:, 1] = term_v[:, :256].astype(BF).reshape(4, 192, 256)
     ya = y_send(2, ysend_a, yrecv_a)
-    ysend_b[:, 0] = term_k[:, 256:].reshape(4, 192, 128)
-    ysend_b[:, 1] = term_v[:, 256:].reshape(4, 192, 128)
-    yb = y_send(3, ysend_b, yrecv_b)
-
+
+    def z_made(n, source, landing):
+        out = []
+        for d in FAR_FIRST:
+            block = lax.rem(lax.div(z_peer[d], 8), 8)
+            out.append(made(source.at[block], landing.at[d], z_s.at[n, d], z_r.at[n, d], z_peer[d]))
+        return out
+
+    def z_send(n, source, landing):
+        copies = z_made(n, source, landing)
+        begin(copies)
+        sent.extend(copies)
+        return copies
+
+    def z_blocks(pieces, m):
+        return jnp.concatenate([piece[24 * m : 24 * m + 24] for piece in pieces], 0).astype(BF)
+
+    quarters = [term[192 * n : 192 * n + 192, 256:] for term in (term_k, term_v) for n in range(4)]
+    for m in range(8):
+        zsend_b[m] = z_blocks(quarters, m)
+    zb = z_send(2, zsend_b, zrecv_b)
+
+    y_after_x(1)
     def token_part(which):
         out = mm(gbuf[0, 0], wqkv[0, head_rows(which), :], NT)
         out = out + mm(gbuf[1, 0], wqkv[1, head_rows(which), :], NT)
@@ -463,80 +550,81 @@
     gtok_out[...] = token_part(other_head).astype(BF)
     gtok_copy = push(gtok_out, gtok_in, head_s.at[2], head_r.at[2], seq, other_head)
 
-    def z_send(n, total, source, landing):
+    own_tokens = token_part(head)
+    arrive(ya)
+    totals = y_total(ysend_a[y_at], yrecv_a)
+    for m in range(8):
+        zsend_a[m] = z_blocks([totals[0], totals[1]], m)
+    za = z_send(1, zsend_a, zrecv_a)
+    z_early = z_made(0, zsend, zrecv)
+    f_copy = made(fbuf.at[0], fbuf.at[1], sib_s.at[10], sib_r.at[10], sibling)
+
+    @pl.when(reducer)
+    def _():
+        arrive(y_early[0])
+        arrive(y_early[1])
+        totals = [y_total(ysend[p, y_at], yrecv.at[p]) for p in range(2)]
         for m in range(8):
-            rows = slice(24 * m, 24 * m + 24)
-            source[m] = jnp.concatenate([total[0][rows], total[1][rows]], 0).astype(BF)
-        out = []
-        for d in range(1, 8):
-            block = lax.rem(lax.div(z_peer[d], 8), 8)
-            out.append(
-                push(source.at[block], landing.at[d], z_s.at[n, d], z_r.at[n, d], z_peer[d])
-            )
-        return out
-
-    def y_total(own, landing):
-        out = own.astype(F32)
-        for d in range(1, 4):
-            out = out + landing[d].astype(F32)
-        return out
-
-    def z_total(own, landing):
-        out = own.astype(F32)
-        for d in range(1, 8):
-            out = out + landing[d].astype(F32)
-        return out
-
-    def arrive(copies):
-        for copy in copies:
-            copy.wait_recv()
-
-    def x_send(r):
-        return [
-            push(xbuf.at[r], xrecv.at[r, d], x_s.at[r, d], x_r.at[r, d], cross_peer[d])
-            for d in range(1, 4)
-        ]
-
-    arrive(yw)
-    arrive(yq)
-    totals = [y_total(ysend[p, y_at], yrecv.at[p]) for p in range(2)]
-    z0 = z_send(0, totals, zsend, zrecv)
-    arrive(ya)
-    za = z_send(1, y_total(ysend_a[y_at], yrecv_a), zsend_a, zrecv_a)
-    arrive(yb)
-    zb = z_send(2, y_total(ysend_b[y_at], yrecv_b), zsend_b, zrecv_b)
-    arrive(z0)
-    xbuf[0] = z_total(zsend[z_at], zrecv)
-    x0 = x_send(0)
-    own_tokens = token_part(head)
+            zsend[m] = z_blocks(totals, m)
+        begin(z_early)
+
+    arrive(zb)
+    totals = z_total(zsend_b[z_at], zrecv_b)
+    for n in range(4):
+        ysend_b[n] = jnp.concatenate(
+            [totals[24 * n : 24 * n + 24], totals[96 + 24 * n : 120 + 24 * n]], 0
+        ).astype(BF)
+    yb = y_send(3, ysend_b, yrecv_b)
+    @pl.when(reducer)
+    def _():
+        arrive(z_early)
+        fbuf[0] = z_total(zsend[z_at], zrecv)
+        f_copy.start()
+
     gtok_copy.wait_recv()
     gtok_ref[...] = (own_tokens + gtok_in[...].astype(F32)).astype(BF)
     mixed_copy.wait_recv()
     mixed_ref[...] = (part_a[...] + mixed_in[...].astype(F32)).astype(BF)
+    arrive(yb)
+    xbuf[:, 256:] = y_total(ysend_b[y_at], yrecv_b)
     arrive(za)
-    xbuf[1, :, :256] = z_total(zsend_a[z_at], zrecv_a)
-    arrive(zb)
-    xbuf[1, :, 256:] = z_total(zsend_b[z_at], zrecv_b)
-    x1 = x_send(1)
-
-    def finish(r, copies):
-        arrive(copies)
-        straight = xbuf[r] + xrecv[r, 2]
-        crossed = xrecv[r, 1] + xrecv[r, 3]
-        total = jnp.where(core == x_at, straight, crossed)
+    xbuf[:, :256] = z_total(zsend_a[z_at], zrecv_a)
+    x1 = [
+        push(xbuf, xrecv.at[d], x_s.at[d], x_r.at[d], cross_peer[d]) for d in range(1, 4)
+    ]
+
+    def finish(total):
         return [
             jnp.where(first, total[24 * n : 24 * n + 12], total[24 * n + 12 : 24 * n + 24])
             for n in range(2)
         ]
 
-    one, two = finish(0, x0)
+    @pl.when(jnp.logical_not(reducer))
+    def _():
+        f_copy.wait_recv()
+        fbuf[0] = fbuf[1]
+
+    one, two = finish(fbuf[0])
     gwout_ref[...] = one
     gqkv_ref[0] = two
-    one, two = finish(1, x1)
+    arrive(x1)
+    straight = xbuf[...] + xrecv[2]
+    crossed = xrecv[1] + xrecv[3]
+    one, two = finish(jnp.where(reducer, straight, crossed))
     gqkv_ref[1] = one
     gqkv_ref[2] = two
     for copy in sent:
         copy.wait_send()
+
+    @pl.when(reducer)
+    def _():
+        for copy in y_early[0] + y_early[1] + z_early + [f_copy]:
+            copy.wait_send()
+
+    @pl.when(jnp.logical_not(reducer))
+    def _():
+        for copy in x_copies:
+            copy.wait_send()
 
 
 def finish_kernel(mixed, gtok, gqkv, gwout, mixed_out, gtok_out, gqkv_out, gwout_out):
@@ -580,19 +668,20 @@
         vm((2, WIDTH, WIDTH), BF), vm((WIDTH, WIDTH), BF),
         vm((WIDTH, WIDTH), BF), vm((WIDTH, WIDTH), BF),
         vm((8, 16, WIDTH), BF), vm((8, 16, WIDTH), BF),
-        vm((2, 8, WIDTH), F32), vm((8, WIDTH), F32),
+        vm((2, 8, WIDTH), F32), vm((8, WIDTH), F32), vm((2, 48, ROWS), BF),
+        vm((48, HALF), BF), vm((48, HALF), BF), vm((2, 4, 192, WIDTH), BF), vm((2, 48, WIDTH), F32),
         vm((ROWS, HALF), BF), vm((ROWS, HALF), BF), vm((ROWS, HALF), BF), vm((ROWS, HALF), BF),
         vm((ROWS, HALF), F32),
         vm((2, 4, 192, WIDTH), BF), vm((2, 4, 192, WIDTH), BF),
         vm((4, 2, 192, 256), BF), vm((4, 2, 192, 256), BF),
-        vm((4, 2, 192, 128), BF), vm((4, 2, 192, 128), BF),
+        vm((4, 48, 128), BF), vm((4, 48, 128), BF),
         vm((8, 48, WIDTH), BF), vm((8, 48, WIDTH), BF),
-        vm((8, 48, 256), BF), vm((8, 48, 256), BF), vm((8, 48, 128), BF), vm((8, 48, 128), BF),
-        vm((2, 48, WIDTH), F32), vm((2, 4, 48, WIDTH), F32),
-        dma((6,)), dma((4,)), dma((4,)), dma((10,)), dma((10,)), dma((4,)), dma((4,)),
+        vm((8, 48, 256), BF), vm((8, 48, 256), BF), vm((8, 192, 128), BF), vm((8, 192, 128), BF),
+        vm((48, WIDTH), F32), vm((4, 48, WIDTH), F32),
+        dma((6,)), dma((7,)), dma((7,)), dma((11,)), dma((11,)), dma((4,)), dma((4,)),
         dma((8,)), dma((8,)), dma((8,)), dma((8,)), dma((4,)), dma((4,)),
         dma((8,)), dma((8,)), dma((8,)), dma((8,)), dma((4, 4)), dma((4, 4)),
-        dma((3, 8)), dma((3, 8)), dma((2, 4)), dma((2, 4)),
+        dma((3, 8)), dma((3, 8)), dma((4,)), dma((4,)), dma((2,)), dma((2,)),
     ]
     anywhere = pl.BlockSpec(memory_space=pl.ANY)
     inside = pl.BlockSpec(memory_space=pltpu.VMEM)

time: 97.4 us -> 93.5 us (0.960); the launches traced: 97.3 us -> 92 us
  Pallas kernels: 96.7 us -> 91.4 us
    pallas_call x1, Pallas kernels: 94.6 us -> 89.3 us  [per_device(): pl.pallas_call(kernel, out_shape=(jax.ShapeDtypeStruct((ROWS, HALF), BF),...]
where the time goes in v3:
time: 93.5 us; the launch traced here: 92 us
  Pallas kernels  91.4 us (98%)
    pallas_call x1, Pallas kernels, per_device(): pl.pallas_call(kernel, out_shape=(jax.ShapeDtypeStruct((ROWS, HALF), BF),...  89.3 us
    pallas_call x1, Pallas kernels, per_device(): pl.pallas_call(finish_kernel, out_shape=(jax.ShapeDtypeStruct((ROWS, HALF...  2.05 us

profile of v3, /device:TPU:1, one launch (start us, length us, event | category | flops | bytes accessed | tf_op | source)
XLA Modules:
  0.0 92.0 jit_solution(1644683990664274596)
XLA Ops:
  0.6 89.3 %shard_map.102 = (bf16[256,768]{1,0:T(8,128)(2,1)}, bf16[256,768]{1,0:T(8,128)(2,1)}, f32[3,12,384]{2,1,0:T(8,128)}, f32[12,384]{1,0:T(8,128)}) custom-call(bf16[256,768]{1,0:T(8,128)(2,1)} %tok_hbm.1, bf16[256,768]{1,0:T(8,128)(2,1)} %gout_hbm.1, bf16[3,1536,384]{2,1,0:T(8,128)(2,1)} %bitcast.2, bf16[384,1536]{1,0:T(8,128)(2,1)} %wout_hbm.1, ...), custom_call_target="tpu_custom_call" | custom-call | flops 8000000000 | bytes 12582912 | tf_op jit(solution)/shard_map/pallas_call | solution.py:688
  90.0 2.1 %shard_map.103 = (bf16[256,768]{1,0:T(8,128)(2,1)}, bf16[256,768]{1,0:T(8,128)(2,1)}, f32[12,3,384]{2,1,0:T(4,128)}, f32[12,384]{1,0:T(8,128)}) custom-call(bf16[256,768]{1,0:T(8,128)(2,1)} %get-tuple-element.12.mixed, bf16[256,768]{1,0:T(8,128)(2,1)} %get-tuple-element.13.gtok, f32[3,12,384]{2,1,0:T(8,128)} %get-tuple-element.14.gqkv, ...), custom_call_target="tpu_custom_call" | custom-call | tf_op jit(solution)/shard_map/pallas_call | solution.py:706

commit v4 on v3

--- a/solution.py
+++ b/solution.py
@@ -66,8 +66,8 @@
     return weights, both
 
 
-def level_backward(weights, q_block, grad_block, keys, values, inverse, delta, own_lanes):
-    probs = weights * inverse
+def level_backward(weights, q_block, grad_block, keys, values, total, delta, own_lanes):
+    probs = weights / total
     grad_probs = mm(grad_block, values, NT)
     grad_scores = (probs * (grad_probs - delta)).astype(BF)
     grad_values = mm(probs.astype(BF), grad_block, TN)
@@ -317,15 +317,14 @@
     att_buf[0] = attended
     att_copy = push(att_buf.at[0], att_buf.at[1], sib_s.at[4], sib_r.at[4], sibling)
 
-    inverse = 1.0 / den
     products = grad_att.astype(F32) * attended.astype(F32)
     stat_lane = iota((1, 128), 1)
     stats = jnp.zeros((ROWS, 128), F32)
-    inverses, deltas = [], []
+    row_totals, deltas = [], []
     for h in range(HEADS):
-        inv = inverse[:, 64 * h : 64 * h + 1]
+        inv = den[:, 64 * h : 64 * h + 1]
         delta = jnp.sum(products[:, 64 * h : 64 * h + 64], axis=1, keepdims=True)
-        inverses.append(inv)
+        row_totals.append(inv)
         deltas.append(delta)
         stats = jnp.where(stat_lane == h, inv, stats)
         stats = jnp.where(stat_lane == 8 + h, delta, stats)
@@ -339,7 +338,7 @@
         lanes = iota((rows, 128), 1)
         inv = jnp.sum(jnp.where(lanes == at, got, 0.0), axis=1, keepdims=True)
         delta = jnp.sum(jnp.where(lanes == at + 8, got, 0.0), axis=1, keepdims=True)
-        return inv, delta
+        return jnp.where(inv == 0.0, 1.0, inv), delta
 
     inv, delta = picked_stats(pick23, 8)
     grad_q23, grad_kv = level_backward(
@@ -367,7 +366,7 @@
         parts = []
         for e in range(2):
             h = 2 * p + e
-            probs = w0[h] * inverses[h]
+            probs = w0[h] / row_totals[h]
             grad_probs = mm(grads * side[e], values, NT)
             grad_scores = (probs * (grad_probs - deltas[h])).astype(BF)
             parts.append((

time: 93.5 us -> 93.5 us (level)
  no operation moved by 1% of the time
where the time goes in v4:
time: 93.5 us; the launch traced here: 92 us
  Pallas kernels  91.4 us (98%)
    pallas_call x1, Pallas kernels, per_device(): pl.pallas_call(kernel, out_shape=(jax.ShapeDtypeStruct((ROWS, HALF), BF),...  89.3 us
    pallas_call x1, Pallas kernels, per_device(): pl.pallas_call(finish_kernel, out_shape=(jax.ShapeDtypeStruct((ROWS, HALF...  2.05 us

profile of v4, /device:TPU:1, one launch (start us, length us, event | category | flops | bytes accessed | tf_op | source)
XLA Modules:
  0.0 92.0 jit_solution(7771218622281850091)
XLA Ops:
  0.6 89.3 %shard_map.102 = (bf16[256,768]{1,0:T(8,128)(2,1)}, bf16[256,768]{1,0:T(8,128)(2,1)}, f32[3,12,384]{2,1,0:T(8,128)}, f32[12,384]{1,0:T(8,128)}) custom-call(bf16[256,768]{1,0:T(8,128)(2,1)} %tok_hbm.1, bf16[256,768]{1,0:T(8,128)(2,1)} %gout_hbm.1, bf16[3,1536,384]{2,1,0:T(8,128)(2,1)} %bitcast.2, bf16[384,1536]{1,0:T(8,128)(2,1)} %wout_hbm.1, ...), custom_call_target="tpu_custom_call" | custom-call | flops 8000000000 | bytes 12582912 | tf_op jit(solution)/shard_map/pallas_call | solution.py:687
  90.0 2.1 %shard_map.103 = (bf16[256,768]{1,0:T(8,128)(2,1)}, bf16[256,768]{1,0:T(8,128)(2,1)}, f32[12,3,384]{2,1,0:T(4,128)}, f32[12,384]{1,0:T(8,128)}) custom-call(bf16[256,768]{1,0:T(8,128)(2,1)} %get-tuple-element.12.mixed, bf16[256,768]{1,0:T(8,128)(2,1)} %get-tuple-element.13.gtok, f32[3,12,384]{2,1,0:T(8,128)} %get-tuple-element.14.gqkv, ...), custom_call_target="tpu_custom_call" | custom-call | tf_op jit(solution)/shard_map/pallas_call | solution.py:705
